TPU v7x, 256 devices: a whole 4x4x8 slice. The times are simulated.
256 devices in a mesh: seq: 32 (over y, z), head: 8 (over x, core).
Axes of the slice: x: 4, y: 4, z: 8, core: 2. Of those that a mesh axis runs over, the one named last changes fastest.
Arguments:
- teacher_query: bfloat16 [4096, 4096], P('seq', 'head')
- teacher_key: bfloat16 [4096, 4096], P('seq', 'head')
- teacher_value: bfloat16 [4096, 4096], P('seq', 'head')
- student_hidden: bfloat16 [4096, 2048], P('seq')
- weight_query: bfloat16 [2048, 1024], P(None, 'head'), may hold values from -0.125 to 0.125
- weight_key: bfloat16 [2048, 1024], P(None, 'head'), may hold values from -0.125 to 0.125
- weight_value: bfloat16 [2048, 1024], P(None, 'head'), may hold values from -0.125 to 0.125
- teacher_shift: int32 [1], replicated, may hold values from 128 to 383
- student_shift: int32 [1], replicated, may hold values from 32 to 95
- segment_lengths: int32 [4], replicated, may hold values from 1 to 3072, 4096 in all
Outputs:
- mean_divergence: float32 [], replicated
- gradient_query: bfloat16 [2048, 1024], P('seq', 'head')
- gradient_key: bfloat16 [2048, 1024], P('seq', 'head')
- gradient_value: bfloat16 [2048, 1024], P('seq', 'head')
Inputs may be any that keep to these rules, and one draw needn't show every extreme that they name: teacher_shift lies in 0 .. 511. student_shift lies in 0 .. 127. `segment_lengths`: the lengths sum to 4096; the largest is exactly 3072.
All inputs are finite; a program needn't handle non-finite values.
Results may differ from a plain program's by a relative error of at most 0.0054.
Values may be sent and summed in bfloat16 or wider, within the bound.
A program may use at most 128 MiB of HBM per device.

v0:
```python
import math

import jax
import jax.numpy as jnp
from jax import lax
from jax.sharding import PartitionSpec as P

RT = 256
RS = 64
RH_DEV = 2


NEG = -1e30


def from_behind(array, axis, by):
    size = lax.axis_size(axis)
    return lax.ppermute(array, axis, [(i, (i + by) % size) for i in range(size)])


def document_index(positions, segment_lengths):
    ends = jnp.cumsum(segment_lengths)
    return jnp.sum((positions[:, None] >= ends[None, :]).astype(jnp.int32), axis=1)


def allowed_pairs(rows, cols, segment_lengths):
    same = (
        document_index(rows, segment_lengths)[:, None]
        == document_index(cols, segment_lengths)[None, :]
    )
    return jnp.logical_and(same, cols[None, :] <= rows[:, None])


def row_stats(scores, allowed):
    masked = jnp.where(allowed, scores, NEG)
    peak = jnp.max(masked, axis=-1, keepdims=True)
    total = jnp.sum(jnp.exp(masked - peak), axis=-1, keepdims=True)
    return (peak, total)


def normalize(scores, allowed, peak, total):
    masked = jnp.where(allowed, scores, NEG)
    prob = jnp.exp(masked - peak) / total
    logp = masked - peak - jnp.log(total)
    return (prob, logp)


def window_of(mine, following, offset, width):
    joined = jnp.concatenate([mine, following], axis=1)
    return lax.dynamic_slice_in_dim(joined, offset, width, 1)


def local(
    teacher_query,
    teacher_key,
    teacher_value,
    student_hidden,
    weight_query,
    weight_key,
    weight_value,
    teacher_shift,
    student_shift,
    segment_lengths,
):
    tokens = student_hidden.shape[0]
    seq_count = lax.axis_size("seq")
    head_count = lax.axis_size("head")
    seq_total = tokens * seq_count
    cols_t = teacher_query.shape[1]
    cols_s = weight_query.shape[1]
    heads_here = RH_DEV
    coef = 1.0 / (3 * heads_here * head_count)
    scale_t = 1.0 / math.sqrt(RT)
    scale_s = 1.0 / math.sqrt(RS)
    offset_t = teacher_shift[0]
    offset_s = student_shift[0]
    students = [
        jnp.dot(student_hidden, weight, preferred_element_type=jnp.float32).astype(jnp.bfloat16)
        for weight in (weight_query, weight_key, weight_value)
    ]
    shards = jnp.concatenate([teacher_query, teacher_key, teacher_value] + students, axis=1)
    following = from_behind(shards, "head", -1)
    pieces = []
    for kind in range(3):
        lower = kind * cols_t
        pieces.append(
            window_of(
                shards[:, lower : lower + cols_t],
                following[:, lower : lower + cols_t],
                offset_t,
                cols_t,
            )
        )
    for kind in range(3):
        lower = 3 * cols_t + kind * cols_s
        pieces.append(
            window_of(
                shards[:, lower : lower + cols_s],
                following[:, lower : lower + cols_s],
                offset_s,
                cols_s,
            )
        )
    windows = jnp.concatenate(pieces, axis=1)
    gathered = lax.all_gather(windows, "seq", axis=0, tiled=True)
    rows = lax.axis_index("seq") * tokens + jnp.arange(tokens, dtype=jnp.int32)
    columns = jnp.arange(seq_total, dtype=jnp.int32)
    allowed = allowed_pairs(rows, columns, segment_lengths)[None]
    divergence = jnp.float32(0.0)
    nears = []
    gmats = []
    owns_s = []
    keys_all_t = []
    keys_all_s = []
    owns_t = []
    peaks = []
    totals = []
    for kind in range(3):
        lower_t = kind * cols_t
        lower_s = 3 * cols_t + kind * cols_s
        own_t = windows[:, lower_t : lower_t + cols_t].reshape(tokens, heads_here, RT)
        keys_t = gathered[:, lower_t : lower_t + cols_t].reshape(seq_total, heads_here, RT)
        own_s = windows[:, lower_s : lower_s + cols_s].reshape(tokens, heads_here, RS)
        keys_s = gathered[:, lower_s : lower_s + cols_s].reshape(seq_total, heads_here, RS)
        st = jnp.einsum("ihc,jhc->hij", own_t, keys_t, preferred_element_type=jnp.float32) * scale_t
        ss = jnp.einsum("ihc,jhc->hij", own_s, keys_s, preferred_element_type=jnp.float32) * scale_s
        peak_t, total_t = row_stats(st, allowed)
        peak_s, total_s = row_stats(ss, allowed)
        prob_t, logp_t = normalize(st, allowed, peak_t, total_t)
        prob_s, logp_s = normalize(ss, allowed, peak_s, total_s)
        divergence = divergence + jnp.sum(
            jnp.where(allowed, prob_t * (logp_t - logp_s), jnp.float32(0.0))
        )
        gmat = (jnp.where(allowed, prob_s - prob_t, jnp.float32(0.0)) * coef).astype(jnp.bfloat16)
        nears.append(jnp.einsum("hij,jhc->ihc", gmat, keys_s, preferred_element_type=jnp.float32))
        gmats.append(gmat)
        owns_s.append(own_s)
        owns_t.append(own_t)
        keys_all_t.append(keys_t)
        keys_all_s.append(keys_s)
        peaks.append(peak_t[:, :, 0].T)
        peaks.append(peak_s[:, :, 0].T)
        totals.append(total_t[:, :, 0].T)
        totals.append(total_s[:, :, 0].T)
    partial_terms = jnp.concatenate(
        [
            jnp.einsum(
                "hij,ihc->jhc", gmats[kind], owns_s[kind], preferred_element_type=jnp.float32
            ).reshape(seq_total, cols_s)
            for kind in range(3)
        ],
        axis=1,
    )
    far_terms = lax.psum_scatter(partial_terms, "seq", scatter_dimension=0, tiled=True)
    fars = [
        far_terms[:, kind * cols_s : (kind + 1) * cols_s].reshape(tokens, heads_here, RS)
        for kind in range(3)
    ]
    gradient_window = jnp.concatenate(
        [
            ((nears[kind] + fars[kind]) * scale_s).astype(jnp.bfloat16).reshape(tokens, cols_s)
            for kind in range(3)
        ],
        axis=1,
    )
    previous = from_behind(gradient_window, "head", 1)
    placed = []
    for kind in range(3):
        lower = kind * cols_s
        joined = jnp.concatenate(
            [previous[:, lower : lower + cols_s], gradient_window[:, lower : lower + cols_s]],
            axis=1,
        )
        placed.append(lax.dynamic_slice_in_dim(joined, cols_s - offset_s, cols_s, 1))
    student_grads = jnp.concatenate(placed, axis=1)
    summed = lax.psum_scatter(
        lax.dot_general(
            student_hidden,
            student_grads,
            (((0,), (0,)), ((), ())),
            preferred_element_type=jnp.float32,
        ),
        "seq",
        scatter_dimension=0,
        tiled=True,
    )
    total_div = lax.psum(divergence, ("seq", "head"))
    mean_divergence = total_div / (3 * heads_here * head_count * seq_total)
    return (
        mean_divergence,
        summed[:, 0:cols_s].astype(jnp.bfloat16),
        summed[:, cols_s : 2 * cols_s].astype(jnp.bfloat16),
        summed[:, 2 * cols_s : 3 * cols_s].astype(jnp.bfloat16),
    )


def solution(mesh):
    in_specs = (
        P("seq", "head"),
        P("seq", "head"),
        P("seq", "head"),
        P("seq", None),
        P(None, "head"),
        P(None, "head"),
        P(None, "head"),
        P(),
        P(),
        P(),
    )
    out_specs = (P(), P("seq", "head"), P("seq", "head"), P("seq", "head"))
    return jax.shard_map(local, mesh=mesh, in_specs=in_specs, out_specs=out_specs, check_vma=False)
```

profile of v0, /device:TPU:1, one launch (start us, length us, event | category | flops | bytes accessed | tf_op | source)
XLA Modules:
  0.0 735.3 jit_solution(4745376386595986003)
XLA Ops:
  7.2 0.0 copy-start
  7.2 0.0 all-gather.2.cloned.1.call-start
  7.2 1.1 copy.59
  8.3 1.0 copy.57
  9.4 1.0 copy.58
  10.5 1.4 constant_dynamic-update-slice_fusion.2
  11.9 1.4 constant_dynamic-update-slice_fusion.1
  13.3 1.4 constant_dynamic-update-slice_fusion
  14.7 3.3 collective-permute-start
  19.3 4.6 collective-permute-done
  23.9 0.5 constant_dynamic-update-slice_fusion.11
  24.4 0.5 constant_dynamic-update-slice_fusion.10
  24.9 0.5 constant_dynamic-update-slice_fusion.9
  25.5 0.2 constant_dynamic-update-slice_fusion.8
  25.6 0.2 constant_dynamic-update-slice_fusion.7
  25.8 0.2 constant_dynamic-update-slice_fusion.6
  25.9 0.8 copy-done.7
  26.7 0.0 all-gather.2.cloned.1.call-update
  26.7 0.0 reduce-scatter.5.cloned.1.call-start
  26.8 0.2 reduce-window.8
  27.0 0.1 convert_reduce_fusion.1
  27.1 0.1 convert_reduce_fusion
  27.2 0.5 fusion.48
  27.7 145.0 %all-gather.2.cloned.1.call-done = bf16[4096,1920]{0,1:T(8,128)(2,1)} async-done(((bf16[128,1920]{0,1:T(8,128)(2,1)}), bf16[4096,1920]{0,1:T(8,128)(2,1)}) %all-gather.2.cloned.1.call-update) | async-done | bytes 15728656 | tf_op jit(solution)/shard_map/all_gather | solution.py:105
  172.6 9.3 %fusion.107 = (bf16[4096,512]{0,1:T(8,128)(2,1)}, bf16[4096,512]{0,1:T(8,128)(2,1)}, bf16[4096,512]{0,1:T(8,128)(2,1)}) fusion(bf16[4096,1920]{0,1:T(8,128)(2,1)} %all-gather.2.cloned.1.call-done), kind=kLoop, calls=%fused_computation.154 | loop fusion | bytes 25165824 | tf_op jit(solution)/shard_map/slice | solution.py:122
  182.0 6.1 exponential_reduce_fusion.3
  188.1 6.3 fusion.25
  194.4 6.2 exponential_reduce_fusion.5
  200.7 6.3 fusion.24
  207.0 3.4 fusion.18
  210.4 3.2 exponential_reduce_fusion.1
  213.5 0.1 copy-done.1
  213.7 3.1 fusion.106
  216.8 3.8 exponential_reduce_fusion.2
  220.6 4.9 exponential_reduce_fusion.4
  225.5 3.6 exponential_reduce_fusion
  229.1 5.1 fusion.38
  234.2 7.1 fusion.41
  241.3 17.8 %select_reduce_fusion = (f32[]{:T(128)}, f32[]{:T(128)}, f32[]{:T(128)}, f32[2,128,4096]{2,1,0:T(8,128)}) fusion(f32[2,128,4096]{2,1,0:T(8,128)} %get-tuple-element.63, f32[2,128,4096]{2,1,0:T(8,128)} %get-tuple-element.65, f32[2,128]{1,0:T(2,128)S(1)} %log.53, f32[2,128]{1,0:T(2,128)S(1)} %log.52, pred[128,4096]{1,0:T(8,128)(4,1)S(1)} %fusion.48, ...), kind=kOutput, calls=%fused_computation.49 | output fusion | flops 20980220 | bytes 42473484 | tf_op jit(solution)/shard_map/div | solution.py:43
  259.0 7.1 fusion.35
  266.1 2.2 fusion.115
  268.3 0.4 fusion.114
  268.7 0.4 fusion.113
  269.1 3.1 pad_maximum_fusion
  272.2 0.0 reduce-scatter.5.cloned.1.call-update
  272.2 0.0 reduce-scatter.7.cloned.1.call-start
  272.3 218.8 %reduce-scatter.5.cloned.1.call-done = f32[128,384]{0,1:T(8,128)} async-done(((f32[4096,384]{0,1:T(8,128)}), f32[128,384]{0,1:T(8,128)}) %reduce-scatter.5.cloned.1.call-update) | async-done | bytes 196624 | tf_op jit(solution)/shard_map/reduce_scatter | solution.py:154
  491.1 1.1 fusion.110
  492.1 2.8 fusion.57
  494.9 2.1 fusion.56
  497.0 0.8 fusion.55
  497.9 6.2 collective-permute-start.1
  504.1 1.6 collective-permute-done.1
  505.7 0.1 fusion.68
  505.9 0.1 fusion.66
  506.0 2.3 convolution_bitcast_fusion
  508.3 3.5 copy.77
  511.8 0.0 reduce-scatter.7.cloned.1.call-update
  513.8 76.4 %psum.7 = f32[]{:T(128)} all-reduce(f32[]{:T(128)S(6)} %add.52), channel_id=1, replica_groups=mesh['seq'=32,'head'=8] {'seq','head'}, use_global_device_ids=true, to_apply=%region_18.19 | all-reduce | flops 1 | bytes 8 | tf_op jit(solution)/shard_map/psum | solution.py:187
  590.9 133.4 %reduce-scatter.7.cloned.1.call-done = f32[64,384]{1,0:T(8,128)} async-done(((f32[2048,384]{1,0:T(8,128)}), f32[64,384]{1,0:T(8,128)}) %reduce-scatter.7.cloned.1.call-update) | async-done | bytes 98320
  724.3 1.0 copy.78
  725.3 0.7 copy.68
  726.0 0.7 copy.69
  726.7 0.7 copy.70
  (30 shorter events, 0.2 us)
Async XLA Ops:
  7.2 3.3 copy-start
  7.2 19.6 %copy-start.8 = (s32[4]{0:T(128)S(1)}, s32[4]{0:T(128)}, u32[]{:S(2)}) copy-start(s32[4]{0:T(128)} %param.19) | copy-start | bytes 52
  7.2 165.5 %all-gather.2.cloned.1.call-start = ((), (), s32[]{:S(2)}) async-start(), calls=%async_computation.2 | async-start | bytes 16220160 | tf_op jit(solution)/shard_map/all_gather | solution.py:105
  14.7 9.1 %collective-permute-start = (bf16[128,1920]{0,1:T(8,128)(2,1)S(1)}, bf16[128,1920]{0,1:T(8,128)(2,1)S(1)}, u32[]{:S(2)}, u32[]{:S(2)}) collective-permute-start(bf16[128,1920]{0,1:T(8,128)(2,1)S(1)} %get-tuple-element.60), channel_id=1, source_target_pairs={{0,7},{1,0},{2,1},{3,2},{4,3},{5,4},{6,5},{7,6},{8,15},{9,8},{10,9... | collective-permute-start | bytes 1474568 | tf_op jit(solution)/shard_map/ppermute | solution.py:18
  25.9 0.8 copy-start.7
  26.7 464.3 %reduce-scatter.5.cloned.1.call-start = ((), (), s32[]{:S(2)}) async-start(), calls=%async_computation.3 | async-start | bytes 6488064 | tf_op jit(solution)/shard_map/reduce_scatter | solution.py:154
  210.3 3.3 copy-start.1
  216.8 3.8 copy-start.6
  216.8 8.7 %copy-start.4 = (bf16[4096,128]{0,1:T(8,128)(2,1)}, bf16[4096,128]{0,1:T(8,128)(2,1)S(1)}, u32[]{:S(2)}) copy-start(bf16[4096,128]{0,1:T(8,128)(2,1)S(1)} %get-tuple-element.36) | copy-start | bytes 3145732
  266.1 2.6 copy-start.2
  272.2 452.1 %reduce-scatter.7.cloned.1.call-start = ((), (), s32[]{:S(2)}) async-start(), calls=%async_computation.4 | async-start | bytes 3244032
  491.1 5.9 copy-start.3
  491.1 5.9 copy-start.5
  497.9 7.9 %collective-permute-start.1 = (bf16[128,384]{0,1:T(8,128)(2,1)S(1)}, bf16[128,384]{0,1:T(8,128)(2,1)S(1)}, u32[]{:S(2)}, u32[]{:S(2)}) collective-permute-start(bf16[128,384]{0,1:T(8,128)(2,1)S(1)} %pad_maximum_fusion.1), channel_id=1, source_target_pairs={{0,1},{1,2},{2,3},{3,4},{4,5},{5,6},{6,7},{7,0},{8,9},{9,10},{10,1... | collective-permute-start | bytes 294920 | tf_op jit(solution)/shard_map/ppermute | solution.py:18
Sparse Core Ops, SparseCore 0:
  26.9 145.7 all-gather.1
  272.3 218.6 reduce-scatter.4
  512.0 212.2 reduce-scatter.6
where the time goes:
time: 744 us; the launch traced here: 735 us
  waiting for transfers between devices  503 us (68%)
  blocking collectives  76.4 us (10%)
  matrix products  75.1 us (10%)
  other arithmetic  27.2 us (4%)
  local copies, waits for them, and re-layouts  24.3 us (3%)
  between operations  19.3 us (3%)
  starting transfers between devices  9.61 us (1%)
    reduce_scatter x1, waiting for transfers between devices, local(): lax.psum_scatter(partial_terms, 'seq', scatter_dimension=0, tiled=True)  219 us
    all_gather x1, waiting for transfers between devices, local(): gathered = lax.all_gather(windows, 'seq', axis=0, tiled=True)  145 us
    unnamed x4, waiting for transfers between devices  133 us
    psum x1, blocking collectives, local(): total_div = lax.psum(divergence, ('seq', 'head'))  76.4 us
    div x5, matrix products, normalize(): prob = jnp.exp(masked - peak) / total  31.9 us
    div x1, other arithmetic, normalize(): prob = jnp.exp(masked - peak) / total  17.8 us
  transfers between devices with their start and end apart: 5, of which 5 were waited for; matrix products, arithmetic and copies ran while one was open for 0% of the time, Pallas kernels for 0%

commit v1 on v0

v1 whole, which is shorter than its diff:
```python
import functools
import math

import jax
import jax.numpy as jnp
from jax import lax
from jax.experimental import pallas as pl
from jax.experimental.pallas import tpu as pltpu
from jax.sharding import PartitionSpec as P

MESH = pl.DeviceIdType.MESH
NEG = -1e30
TOK = 128
NZ = 8
NY = 4
PAIRS = 6
SLOTS = NY * NZ
PIECE = 320
ROWS = 256
CHUNK = 512
KEYS = SLOTS * TOK
F32 = jnp.float32
BF16 = jnp.bfloat16


def place():
    seq = lax.axis_index("seq")
    head = lax.axis_index("head")
    return seq, head, seq // NZ, seq % NZ, head // 2, head % 2


def greet(peers):
    barrier = pltpu.get_barrier_semaphore()
    for peer in peers:
        pl.semaphore_signal(barrier, inc=1, device_id=peer, device_id_type=MESH)
    return lambda: pl.semaphore_wait(barrier, len(peers))


def remote(src, dst, send, recv, device):
    return pltpu.make_async_remote_copy(
        src_ref=src, dst_ref=dst, send_sem=send, recv_sem=recv, device_id=device, device_id_type=MESH
    )


def swap_halves(x):
    return pltpu.roll(x, 64, 1)


def low_lanes(shape):
    return lax.broadcasted_iota(jnp.int32, shape, 1) < 64


def spread_kernel(
    t_shift, s_shift, tq, tk, tv, hidden, wq, wk, wv,
    keys, cols,
    near_a, near_b, near_s, stud, piece, transit, hid,
    a_send, a_recv, b_send, b_recv, s_send, s_recv,
    p_send, key_sem, tr_sem, f_send, g_send, r_send, h_send, h_recv,
):
    seq, head, y, z, x, c = place()
    sibling = (seq, head + 1 - 2 * c)
    behind = (seq, (head + 7) % 8)
    peers = [sibling]
    for dz in range(1, NZ):
        other = y * NZ + (z + dz) % NZ
        peers.append((other, head))
        peers.append((other, sibling[1]))
    for dy in range(1, NY):
        peers.append((((y + dy) % NY) * NZ + z, head))
    peers.append((seq, (head + 7 + 2 * c) % 8))
    wait_all = greet(peers)

    for kind, weight in enumerate((wq, wk, wv)):
        stud[:, kind * 128 : (kind + 1) * 128] = jnp.dot(
            hidden[...], weight[...], preferred_element_type=F32
        ).astype(BF16)
    wait_all()

    teachers = (tq, tk, tv)
    outs = []
    for kind in range(3):
        outs.append(remote(teachers[kind].at[:, 0:128], near_a.at[kind], a_send.at[kind], a_recv.at[kind], behind))
    out_s = remote(stud, near_s, s_send, s_recv, behind)
    for kind in range(3):
        outs.append(remote(teachers[kind].at[:, 128:384], near_b.at[kind], b_send.at[kind], b_recv.at[kind], behind))
    for copy in outs[:3]:
        copy.start()
    out_s.start()
    for copy in outs[3:]:
        copy.start()

    def one_hot(rows, columns, first):
        there = lax.broadcasted_iota(jnp.int32, (rows, columns), 0)
        here = lax.broadcasted_iota(jnp.int32, (rows, columns), 1)
        return jnp.where(there == here + first, jnp.float32(1.0), jnp.float32(0.0)).astype(BF16)

    pick_t = one_hot(512, 256, t_shift[0] - 128)
    pick_s = one_hot(256, 128, s_shift[0])
    own_pair = c == y // 2
    core = z % 2

    def send_piece(k, go):
        target = (y * NZ + k, 2 * x + core)
        mine = jnp.logical_and(z == k, core == c)
        away = jnp.logical_not(mine)

        @pl.when(jnp.logical_and(own_pair, away))
        def _():
            copy = remote(piece.at[k], keys.at[seq], p_send.at[k], key_sem.at[seq], target)
            copy.start() if go else copy.wait_send()

        @pl.when(jnp.logical_and(jnp.logical_not(own_pair), away))
        def _():
            copy = remote(piece.at[k], transit.at[z // 2], p_send.at[k], tr_sem.at[z // 2], target)
            copy.start() if go else copy.wait_send()

        if go:
            @pl.when(jnp.logical_and(own_pair, mine))
            def _():
                pltpu.make_async_copy(piece.at[k], keys.at[seq], key_sem.at[seq]).start()

            @pl.when(jnp.logical_and(jnp.logical_not(own_pair), mine))
            def _():
                pltpu.make_async_copy(piece.at[k], transit.at[z // 2], tr_sem.at[z // 2]).start()

    low = low_lanes((64, 128))
    for j in range(2):
        for kind in range(3):
            if j == 0:
                outs[kind].wait_recv()
                if kind == 0:
                    out_s.wait_recv()
                window = jnp.dot(
                    teachers[kind][:, 128:512], pick_t[0:384], preferred_element_type=F32
                ) + jnp.dot(near_a[kind], pick_t[384:512], preferred_element_type=F32)
            else:
                outs[3 + kind].wait_recv()
                window = (
                    jnp.dot(teachers[kind][:, 384:512], pick_t[0:128], preferred_element_type=F32)
                    + jnp.dot(near_a[kind], pick_t[128:256], preferred_element_type=F32)
                    + jnp.dot(near_b[kind], pick_t[256:512], preferred_element_type=F32)
                )
            at = slice(kind * 128, (kind + 1) * 128)
            small = jnp.dot(stud[:, at], pick_s[0:128], preferred_element_type=F32) + jnp.dot(
                near_s[:, at], pick_s[128:256], preferred_element_type=F32
            )
            k = kind * 2 + j
            piece[k, 0:128] = window[:, 0:128].astype(BF16)
            piece[k, 128:256] = window[:, 128:256].astype(BF16)
            if j == 0:
                packed = jnp.where(low, small[0:64], swap_halves(small[64:128]))
            else:
                packed = jnp.where(low, swap_halves(small[0:64]), small[64:128])
            piece[k, 256:320] = packed.astype(BF16)
            send_piece(k, True)

    for part in range(4):
        for block in range(4):
            hid[part, :, block * 128 : (block + 1) * 128] = hidden[
                :, block * 512 + part * 128 : block * 512 + part * 128 + 128
            ]

    active = z < PAIRS

    def key_copy(slot, send, device):
        return remote(keys.at[slot], keys.at[slot], send, key_sem.at[slot], device)

    partner = ((y + 1 - 2 * (y % 2)) * NZ + z, head)
    far_row = 2 * (1 - y // 2)

    def forwards(i):
        slot = y * NZ + 2 * i + c
        first = key_copy(slot, f_send.at[i], partner)
        relay = key_copy(slot, r_send.at[i], sibling)
        others = [
            remote(transit.at[i], keys.at[slot], g_send.at[2 * i + b], key_sem.at[slot], ((far_row + b) * NZ + z, head))
            for b in range(2)
        ]
        return first, relay, others

    @pl.when(active)
    def _():
        for i in range(4):
            first, relay, others = forwards(i)
            remote(transit.at[i], transit.at[i], g_send.at[2 * i], tr_sem.at[i], partner).wait_recv()
            for copy in others:
                copy.start()
            first.wait_recv()
            first.start()
            relay.start()

    columns_out = []
    for d in range(1, 4):
        to = (z + 2 * d) % NZ
        columns_out.append(
            remote(hid.at[to // 2], cols.at[z // 2], h_send.at[d], h_recv.at[z // 2], (y * NZ + to, head))
        )
    for copy in columns_out:
        copy.start()
    own_cols = pltpu.make_async_copy(hid.at[z // 2], cols.at[z // 2], h_recv.at[z // 2])
    own_cols.start()

    @pl.when(active)
    def _():
        for i in range(4):
            for n, dy in enumerate((1, 2, 3)):
                other = y // 2 * 2 + 1 - y % 2 if dy == 1 else far_row + dy - 2
                slot = other * NZ + 2 * i + c
                relay = key_copy(slot, r_send.at[4 + 3 * i + n], sibling)
                relay.wait_recv()
                relay.start()
        for i in range(4):
            for row in range(NY):
                slot = row * NZ + 2 * i + 1 - c
                key_copy(slot, r_send.at[0], sibling).wait_recv()
        for i in range(4):
            first, relay, others = forwards(i)
            first.wait_send()
            relay.wait_send()
            for copy in others:
                copy.wait_send()
            for n in range(3):
                key_copy(0, r_send.at[4 + 3 * i + n], sibling).wait_send()

    for part in range(4):
        pltpu.make_async_copy(hid.at[part], cols.at[part], h_recv.at[part]).wait()
    for copy in columns_out:
        copy.wait_send()
    for copy in outs:
        copy.wait_send()
    out_s.wait_send()
    for k in range(PAIRS):
        send_piece(k, False)


def spread(t_shift, s_shift, tq, tk, tv, hidden, wq, wk, wv):
    vmem = pl.BlockSpec(memory_space=pltpu.VMEM)
    smem = pl.BlockSpec(memory_space=pltpu.SMEM)
    dma = pltpu.SemaphoreType.DMA
    return pl.pallas_call(
        spread_kernel,
        name="spread",
        out_shape=(
            jax.ShapeDtypeStruct((SLOTS, PIECE, 128), BF16),
            jax.ShapeDtypeStruct((4, TOK, 512), BF16),
        ),
        in_specs=[smem, smem] + [vmem] * 7,
        out_specs=(pl.BlockSpec(memory_space=pl.ANY), pl.BlockSpec(memory_space=pl.ANY)),
        scratch_shapes=[
            pltpu.VMEM((3, TOK, 128), BF16),
            pltpu.VMEM((3, TOK, 256), BF16),
            pltpu.VMEM((TOK, 384), BF16),
            pltpu.VMEM((TOK, 384), BF16),
            pltpu.VMEM((PAIRS, PIECE, 128), BF16),
            pltpu.VMEM((4, PIECE, 128), BF16),
            pltpu.VMEM((4, TOK, 512), BF16),
            dma((3,)), dma((3,)), dma((3,)), dma((3,)), dma(()), dma(()),
            dma((PAIRS,)), dma((SLOTS,)), dma((4,)), dma((4,)), dma((8,)), dma((16,)), dma((4,)), dma((4,)),
        ],
        compiler_params=pltpu.CompilerParams(
            collective_id=0, has_side_effects=True, vmem_limit_bytes=32 * 1024 * 1024
        ),
    )(t_shift, s_shift, tq, tk, tv, hidden, wq, wk, wv)


def relate_kernel(where, lengths, keys, part, div, kt, ks, st, ss, acc, top_t, top_s, row_t, row_s, near):
    seq = where[0]
    c = where[1] % 2
    y = seq // NZ
    z = seq % NZ
    group = 2 * (y % 2) + c
    div[...] = jnp.zeros_like(div)
    coef = jnp.float32(1.0 / 48.0)
    scale_t = jnp.float32(1.0 / 16.0)
    scale_s = jnp.float32(1.0 / 8.0)
    sub = 32

    @pl.when(z < PAIRS)
    def _():
        low = low_lanes((64, 128))

        @pl.loop(0, SLOTS)
        def _(slot):
            base = pl.multiple_of(slot * TOK, TOK)
            kt[pl.ds(base, TOK), 0:128] = keys[slot, 0:128]
            kt[pl.ds(base, TOK), 128:256] = keys[slot, 128:256]
            packed = keys[slot, 256:320].astype(F32)
            zero = jnp.zeros_like(packed)
            ks[pl.ds(base, 64)] = jnp.where(low, packed, zero).astype(BF16)
            ks[pl.ds(base + 64, 64)] = jnp.where(low, swap_halves(packed), zero).astype(BF16)

        acc[...] = jnp.zeros_like(acc)
        end0 = lengths[0]
        end1 = end0 + lengths[1]
        end2 = end1 + lengths[2]

        def first_of(position):
            zero = jnp.int32(0)
            start = jnp.where(position >= end0, end0, zero)
            start = jnp.where(position >= end1, end1, start)
            return jnp.where(position >= end2, end2, start)

        @pl.loop(0, 4)
        def _(t):
            odd = t % 2
            block = 4 * t + odd * 3 + (1 - 2 * odd) * group
            r0 = pl.multiple_of(block * ROWS, ROWS)
            lower = first_of(r0) // CHUNK
            upper = (r0 + ROWS - 1) // CHUNK + 1
            top_t[...] = jnp.full_like(top_t, NEG)
            top_s[...] = jnp.full_like(top_s, NEG)

            @pl.loop(lower, upper)
            def _(n):
                k0 = pl.multiple_of(n * CHUNK, CHUNK)
                dims = (((1,), (1,)), ((), ()))
                st[:, pl.ds(k0, CHUNK)] = lax.dot_general(
                    kt[pl.ds(r0, ROWS)], kt[pl.ds(k0, CHUNK)], dims, preferred_element_type=F32
                )
                ss[:, pl.ds(k0, CHUNK)] = lax.dot_general(
                    ks[pl.ds(r0, ROWS)], ks[pl.ds(k0, CHUNK)], dims, preferred_element_type=F32
                )

                @pl.loop(0, ROWS // sub)
                def _(r):
                    at = pl.multiple_of(r * sub, sub)
                    row = r0 + at + lax.broadcasted_iota(jnp.int32, (sub, 128), 0)
                    start = first_of(row)
                    mt = top_t[pl.ds(at, sub)]
                    ms = top_s[pl.ds(at, sub)]
                    for q in range(CHUNK // 128):
                        c0 = pl.multiple_of(k0 + q * 128, 128)
                        column = c0 + lax.broadcasted_iota(jnp.int32, (sub, 128), 1)
                        allowed = jnp.logical_and(column >= start, column <= row)
                        a = jnp.where(allowed, st[pl.ds(at, sub), pl.ds(c0, 128)] * scale_t, NEG)
                        b = jnp.where(allowed, ss[pl.ds(at, sub), pl.ds(c0, 128)] * scale_s, NEG)
                        st[pl.ds(at, sub), pl.ds(c0, 128)] = a
                        ss[pl.ds(at, sub), pl.ds(c0, 128)] = b
                        mt = jnp.maximum(mt, a)
                        ms = jnp.maximum(ms, b)
                    top_t[pl.ds(at, sub)] = mt
                    top_s[pl.ds(at, sub)] = ms

            @pl.loop(0, ROWS // sub)
            def _(r):
                at = pl.multiple_of(r * sub, sub)
                mt = jnp.max(top_t[pl.ds(at, sub)], axis=1, keepdims=True)
                ms = jnp.max(top_s[pl.ds(at, sub)], axis=1, keepdims=True)
                zero = jnp.zeros((sub, 128), F32)

                def body(n, carry):
                    tot_t, tot_s, cross = carry
                    k0 = pl.multiple_of(n * CHUNK, CHUNK)
                    for q in range(CHUNK // 128):
                        c0 = pl.multiple_of(k0 + q * 128, 128)
                        a = st[pl.ds(at, sub), pl.ds(c0, 128)]
                        b = ss[pl.ds(at, sub), pl.ds(c0, 128)]
                        ea = jnp.exp(a - mt)
                        eb = jnp.exp(b - ms)
                        st[pl.ds(at, sub), pl.ds(c0, 128)] = ea
                        ss[pl.ds(at, sub), pl.ds(c0, 128)] = eb
                        tot_t = tot_t + ea
                        tot_s = tot_s + eb
                        cross = cross + ea * (a - b)
                    return tot_t, tot_s, cross

                tot_t, tot_s, cross = lax.fori_loop(lower, upper, body, (zero, zero, zero))
                tot_t = jnp.sum(tot_t, axis=1, keepdims=True)
                tot_s = jnp.sum(tot_s, axis=1, keepdims=True)
                cross = jnp.sum(cross, axis=1, keepdims=True)
                value = cross / tot_t + (ms + jnp.log(tot_s)) - (mt + jnp.log(tot_t))
                spread_value = jnp.broadcast_to(value * jnp.float32(1.0 / 128.0), (sub, 128))
                add = spread_value[0:8]
                for m in range(1, sub // 8):
                    add = add + spread_value[8 * m : 8 * m + 8]
                div[...] += add
                row_t[pl.ds(at, sub)] = jnp.broadcast_to(coef / tot_t, (sub, 128))
                row_s[pl.ds(at, sub)] = jnp.broadcast_to(coef / tot_s, (sub, 128))

            near[...] = jnp.zeros_like(near)

            @pl.loop(lower, upper)
            def _(n):
                k0 = pl.multiple_of(n * CHUNK, CHUNK)
                wide_t = jnp.concatenate([row_t[...]] * (CHUNK // 128), axis=1)
                wide_s = jnp.concatenate([row_s[...]] * (CHUNK // 128), axis=1)
                g = (ss[:, pl.ds(k0, CHUNK)] * wide_s - st[:, pl.ds(k0, CHUNK)] * wide_t).astype(BF16)
                near[...] += jnp.dot(g, ks[pl.ds(k0, CHUNK)], preferred_element_type=F32)
                acc[pl.ds(k0, CHUNK)] += lax.dot_general(
                    g, ks[pl.ds(r0, ROWS)], (((0,), (0,)), ((), ())), preferred_element_type=F32
                )

            acc[pl.ds(r0, ROWS)] += near[...]

        for row in range(NY):
            for parity in range(2):
                for i in range(4):
                    base = (row * NZ + 2 * i + parity) * TOK
                    part[row, parity, i] = (
                        jnp.where(low, acc[base : base + 64], swap_halves(acc[base + 64 : base + 128])) * scale_s
                    ).astype(BF16)


def relate(where, lengths, keys):
    vmem = pl.BlockSpec(memory_space=pltpu.VMEM)
    smem = pl.BlockSpec(memory_space=pltpu.SMEM)
    return pl.pallas_call(
        relate_kernel,
        name="relate",
        out_shape=(
            jax.ShapeDtypeStruct((NY, 2, 4, 64, 128), BF16),
            jax.ShapeDtypeStruct((8, 128), F32),
        ),
        in_specs=[smem, smem, vmem],
        out_specs=(vmem, vmem),
        scratch_shapes=[
            pltpu.VMEM((KEYS, 256), BF16),
            pltpu.VMEM((KEYS, 128), BF16),
            pltpu.VMEM((ROWS, KEYS), F32),
            pltpu.VMEM((ROWS, KEYS), F32),
            pltpu.VMEM((KEYS, 128), F32),
            pltpu.VMEM((ROWS, 128), F32),
            pltpu.VMEM((ROWS, 128), F32),
            pltpu.VMEM((ROWS, 128), F32),
            pltpu.VMEM((ROWS, 128), F32),
            pltpu.VMEM((ROWS, 128), F32),
        ],
        compiler_params=pltpu.CompilerParams(vmem_limit_bytes=40 * 1024 * 1024),
    )(where, lengths, keys)


def fold_kernel(
    s_shift, part, div, cols,
    mean, gq, gk, gv,
    in1, sums, in2, db, outp, in4, win, prev, div_a, div_b, div_c, div_1, div_2,
    s1, r1, s2, r2, s4, r4, sw, rw, sa, ra, sb, rb, sc, rc,
):
    seq, head, y, z, x, c = place()
    ahead = (seq, (head + 1) % 8)
    other = head + 1 - 2 * c
    peers = [(seq, (head + d) % 8) for d in range(1, 8)]
    for dz in range(1, NZ):
        for h in (head, other):
            peers.append((y * NZ + (z + dz) % NZ, h))
    for dy in range(1, NY):
        for h in (head, other):
            peers.append((((y + dy) % NY) * NZ + z, h))
        peers.append((((y + dy) % NY) * NZ + z + 1 - 2 * (z % 2), head))
    greet(peers)()
    active = z < PAIRS

    def row_copies():
        me = y * 2 + c
        copies = []
        for dy in range(1, NY):
            row = (y + dy) % NY
            for core in range(2):
                copies.append(
                    remote(part.at[row, core], in1.at[me], s1.at[2 * dy + core], r1.at[me], (row * NZ + z, 2 * x + core))
                )
        copies.append(remote(part.at[y, 1 - c], in1.at[me], s1.at[0], r1.at[me], (seq, other)))
        return copies

    own_div = pltpu.make_async_copy(div, div_a.at[y], ra.at[y])
    own_div.start()
    div_row = [
        remote(div, div_a.at[y], sa.at[dy], ra.at[y], (((y + dy) % NY) * NZ + z, head)) for dy in range(1, NY)
    ]

    @pl.when(active)
    def _():
        pltpu.make_async_copy(part.at[y, c], in1.at[y * 2 + c], r1.at[y * 2 + c]).start()
        for copy in row_copies():
            copy.start()

    for copy in div_row:
        copy.start()

    def pair_copies(p):
        copies = []
        for i in range(4):
            copies.append((i, remote(sums.at[p], in2.at[z], s2.at[p * 4 + i], r2.at[z], (y * NZ + 2 * i + c, 2 * x + p))))
        return copies

    def each_pair_copy(p, go):
        for i, copy in pair_copies(p):
            mine = jnp.logical_and(z == 2 * i + c, c == p)

            @pl.when(jnp.logical_not(mine))
            def _():
                copy.start() if go else copy.wait_send()

            if go:
                @pl.when(mine)
                def _():
                    pltpu.make_async_copy(sums.at[p], in2.at[z], r2.at[z]).start()

    @pl.when(active)
    def _():
        for p in range(2):
            total = jnp.zeros((4, 64, 128), F32)
            for n in range(4):
                pltpu.make_async_copy(in1.at[4 * p + n], in1.at[4 * p + n], r1.at[4 * p + n]).wait()
                total = total + in1[4 * p + n].astype(F32)
            sums[p] = total.astype(BF16)
            each_pair_copy(p, True)

    for n in range(NY):
        pltpu.make_async_copy(div_a.at[n], div_a.at[n], ra.at[n]).wait()
    div_1[...] = (div_a[0] + div_a[1]) + (div_a[2] + div_a[3])
    pltpu.make_async_copy(div_1, div_b.at[z], rb.at[z]).start()
    div_col = [
        remote(div_1, div_b.at[z], sb.at[dz], rb.at[z], (y * NZ + (z + dz) % NZ, head)) for dz in range(1, NZ)
    ]
    for copy in div_col:
        copy.start()

    def eight(buf):
        return ((buf[0] + buf[1]) + (buf[2] + buf[3])) + ((buf[4] + buf[5]) + (buf[6] + buf[7]))

    for n in range(NZ):
        pltpu.make_async_copy(div_b.at[n], div_b.at[n], rb.at[n]).wait()
    div_2[...] = eight(div_b)
    pltpu.make_async_copy(div_2, div_c.at[head], rc.at[head]).start()
    div_head = [
        remote(div_2, div_c.at[head], sc.at[d], rc.at[head], (seq, (head + d) % 8)) for d in range(1, 8)
    ]
    for copy in div_head:
        copy.start()

    low = low_lanes((64, 128))
    for kind in range(3):
        for j in range(2):
            k = 2 * kind + j
            pltpu.make_async_copy(in2.at[k], in2.at[k], r2.at[k]).wait()
        for i in range(4):
            p0 = in2[2 * kind, i].astype(F32)
            p1 = in2[2 * kind + 1, i].astype(F32)
            at = slice(kind * 128, (kind + 1) * 128)
            db[i * 128 : i * 128 + 64, at] = jnp.where(low, p0, swap_halves(p1)).astype(BF16)
            db[i * 128 + 64 : i * 128 + 128, at] = jnp.where(low, swap_halves(p0), p1).astype(BF16)
    grad = jnp.zeros((512, 384), F32)
    for i in range(4):
        grad = grad + lax.dot_general(
            cols[i], db[i * 128 : (i + 1) * 128], (((0,), (0,)), ((), ())), preferred_element_type=F32
        )
    for n in range(8):
        outp[n] = grad[n * 64 : (n + 1) * 64].astype(BF16)

    slot = y * 2 + z % 2
    pltpu.make_async_copy(outp.at[slot], in4.at[slot], r4.at[slot]).start()
    block_copies = []
    for d in range(1, 8):
        to = (slot + d) % 8
        block_copies.append(
            remote(
                outp.at[to], in4.at[slot], s4.at[d], r4.at[slot],
                ((to // 2) * NZ + (z // 2) * 2 + to % 2, head),
            )
        )
    for copy in block_copies:
        copy.start()
    total = jnp.zeros((64, 384), F32)
    for n in range(8):
        pltpu.make_async_copy(in4.at[n], in4.at[n], r4.at[n]).wait()
        total = total + in4[n].astype(F32)
    win[...] = total.astype(BF16)
    last = remote(win, prev, sw, rw, ahead)
    last.start()

    there = lax.broadcasted_iota(jnp.int32, (256, 128), 0)
    here = lax.broadcasted_iota(jnp.int32, (256, 128), 1)
    pick = jnp.where(there == here + (128 - s_shift[0]), jnp.float32(1.0), jnp.float32(0.0)).astype(BF16)
    for n in range(8):
        pltpu.make_async_copy(div_c.at[n], div_c.at[n], rc.at[n]).wait()
    mean[0, 0] = jnp.sum(eight(div_c)) * jnp.float32(1.0 / 196608.0)
    last.wait_recv()
    for kind, out in enumerate((gq, gk, gv)):
        at = slice(kind * 128, (kind + 1) * 128)
        out[...] = (
            jnp.dot(prev[:, at], pick[0:128], preferred_element_type=F32)
            + jnp.dot(win[:, at], pick[128:256], preferred_element_type=F32)
        ).astype(BF16)

    last.wait_send()
    for copy in block_copies + div_head + div_col + div_row:
        copy.wait_send()

    @pl.when(active)
    def _():
        for copy in row_copies():
            copy.wait_send()
        for p in range(2):
            each_pair_copy(p, False)


def fold(s_shift, part, div, cols):
    vmem = pl.BlockSpec(memory_space=pltpu.VMEM)
    smem = pl.BlockSpec(memory_space=pltpu.SMEM)
    dma = pltpu.SemaphoreType.DMA
    grad = jax.ShapeDtypeStruct((64, 128), BF16)
    return pl.pallas_call(
        fold_kernel,
        name="fold",
        out_shape=(jax.ShapeDtypeStruct((1, 1), F32), grad, grad, grad),
        in_specs=[smem, vmem, vmem, vmem],
        out_specs=(smem, vmem, vmem, vmem),
        scratch_shapes=[
            pltpu.VMEM((8, 4, 64, 128), BF16),
            pltpu.VMEM((2, 4, 64, 128), BF16),
            pltpu.VMEM((PAIRS, 4, 64, 128), BF16),
            pltpu.VMEM((512, 384), BF16),
            pltpu.VMEM((8, 64, 384), BF16),
            pltpu.VMEM((8, 64, 384), BF16),
            pltpu.VMEM((64, 384), BF16),
            pltpu.VMEM((64, 384), BF16),
            pltpu.VMEM((NY, 8, 128), F32),
            pltpu.VMEM((NZ, 8, 128), F32),
            pltpu.VMEM((8, 8, 128), F32),
            pltpu.VMEM((8, 128), F32),
            pltpu.VMEM((8, 128), F32),
            dma((8,)), dma((8,)), dma((8,)), dma((PAIRS,)), dma((8,)), dma((8,)), dma(()), dma(()),
            dma((NY,)), dma((NY,)), dma((NZ,)), dma((NZ,)), dma((8,)), dma((8,)),
        ],
        compiler_params=pltpu.CompilerParams(
            collective_id=1, has_side_effects=True, vmem_limit_bytes=32 * 1024 * 1024
        ),
    )(s_shift, part, div, cols)


def local(
    teacher_query, teacher_key, teacher_value, student_hidden, weight_query, weight_key, weight_value,
    teacher_shift, student_shift, segment_lengths,
):
    keys, cols = spread(
        teacher_shift, student_shift, teacher_query, teacher_key, teacher_value, student_hidden,
        weight_query, weight_key, weight_value,
    )
    where = jnp.stack([lax.axis_index("seq"), lax.axis_index("head")]).astype(jnp.int32)
    part, div = relate(where, segment_lengths, keys)
    mean, gq, gk, gv = fold(student_shift, part, div, cols)
    return mean[0, 0], gq, gk, gv


def solution(mesh):
    in_specs = (
        P("seq", "head"),
        P("seq", "head"),
        P("seq", "head"),
        P("seq", None),
        P(None, "head"),
        P(None, "head"),
        P(None, "head"),
        P(),
        P(),
        P(),
    )
    out_specs = (P(), P("seq", "head"), P("seq", "head"), P("seq", "head"))
    return jax.shard_map(local, mesh=mesh, in_specs=in_specs, out_specs=out_specs, check_vma=False)
```

time: 744 us -> 126 us (0.17); the launches traced: 735 us -> 126 us
  waiting for transfers between devices: 503 us -> 0 us
  Pallas kernels: 0 us -> 112 us
  blocking collectives: 76.4 us -> 0 us
  matrix products: 75.1 us -> 0 us
  other arithmetic: 27.2 us -> 0.08 us
  between operations: 19.3 us -> 3.73 us
  local copies, waits for them, and re-layouts: 24.3 us -> 9.34 us
  starting transfers between devices: 9.61 us -> 0 us
    reduce_scatter x1 -> x0, waiting for transfers between devices: 219 us -> none  [local(): lax.psum_scatter(partial_terms, 'seq', scatter_dimension=0, tiled=True)]
    all_gather x1 -> x0, waiting for transfers between devices: 145 us -> none  [local(): gathered = lax.all_gather(windows, 'seq', axis=0, tiled=True)]
    unnamed x4 -> x0, waiting for transfers between devices: 133 us -> none
    pallas_call x0 -> x3, Pallas kernels: none -> 112 us  [the longest x1 45.5 us: fold(): pl.pallas_call(fold_kernel, name='fold', out_shape=(jax.ShapeDtypeStruct(...]
    psum x1 -> x0, blocking collectives: 76.4 us -> none  [local(): total_div = lax.psum(divergence, ('seq', 'head'))]
    div x5 -> x0, matrix products: 31.9 us -> none  [normalize(): prob = jnp.exp(masked - peak) / total]
    sub x5 -> x0, matrix products: 24.6 us -> none  [the longest x2 12.4 us: normalize(): prob = jnp.exp(masked - peak) / total]
    dot_general x11 -> x0, matrix products: 18.6 us -> none  [the longest x3 5.68 us: local(): jnp.einsum('hij,jhc->ihc', gmat, keys_s, preferred_element_type=jnp.float32)]
  transfers between devices with their start and end apart: 5 -> 0, of which waited for: 5 -> 0; matrix products, arithmetic and copies ran while one was open for 0% -> 0% of each run, Pallas kernels for 0% -> 0%
where the time goes in v1:
time: 126 us
  Pallas kernels  112 us (89%)
  local copies, waits for them, and re-layouts  9.34 us (7%)
  between operations  3.73 us (3%)
    pallas_call x1, Pallas kernels, fold(): pl.pallas_call(fold_kernel, name='fold', out_shape=(jax.ShapeDtypeStruct(...  45.5 us
    pallas_call x1, Pallas kernels, spread(): pl.pallas_call(spread_kernel, name='spread', out_shape=(jax.ShapeDtypeStr...  37.2 us
    pallas_call x1, Pallas kernels, relate(): pl.pallas_call(relate_kernel, name='relate', out_shape=(jax.ShapeDtypeStr...  29.8 us
    unnamed x19, local copies, waits for them, and re-layouts  9.34 us

profile of v1, /device:TPU:1, one launch (start us, length us, event | category | flops | bytes accessed | tf_op | source)
XLA Modules:
  0.0 125.6 jit_solution(2563958011656294346)
XLA Ops:
  1.9 0.1 pad_add_fusion.where
  2.0 0.0 copy-start
  2.0 1.0 copy-done
  3.0 0.0 copy-start.1
  3.0 1.0 copy-done.1
  4.1 0.0 copy-start.2
  4.1 1.0 copy-done.2
  5.1 0.0 copy-start.3
  5.1 1.0 copy-done.3
  6.2 0.0 copy-start.4
  6.2 0.9 copy-done.4
  7.1 0.0 copy-start.5
  7.1 0.9 copy-done.5
  8.0 0.0 copy-start.6
  8.0 0.9 copy-done.6
  8.9 37.2 %spread.1 = (bf16[32,320,128]{2,1,0:T(8,128)(2,1)S(1)}, bf16[4,128,512]{2,1,0:T(8,128)(2,1)S(1)}) custom-call(s32[1]{0:T(128)S(6)} %copy.18.t_shift, s32[1]{0:T(128)S(6)} %copy.19.s_shift, bf16[128,512]{1,0:T(8,128)(2,1)S(1)} %copy-done.4, bf16[128,512]{1,0:T(8,128)(2,1)S(1)} %copy-done.5, bf16[128,512]{1,0:T(8,128)(2,1)S(1)} %copy-done.6, ...), custom_call_target="tpu_custom_call" | custom-call | tf_op jit(solution)/shard_map/spread/pallas_call | solution.py:240
  46.1 0.0 copy-start.7
  46.1 0.6 copy-done.7
  46.7 29.8 %relate.1 = (bf16[4,2,4,64,128]{4,3,2,1,0:T(8,128)(2,1)S(1)}, f32[8,128]{1,0:T(8,128)S(1)}) custom-call(s32[2]{0:T(128)S(1)} %pad_add_fusion.where, s32[4]{0:T(128)S(1)} %copy-done.7, bf16[32,320,128]{2,1,0:T(8,128)(2,1)S(1)} %get-tuple-element.12.keys), custom_call_target="tpu_custom_call" | custom-call | tf_op jit(solution)/shard_map/relate/pallas_call | solution.py:407
  76.5 45.5 %fold.1 = (f32[1,1]{1,0:T(1,128)}, bf16[64,128]{1,0:T(8,128)(2,1)S(1)}, bf16[64,128]{1,0:T(8,128)(2,1)S(1)}, bf16[64,128]{1,0:T(8,128)(2,1)S(1)}) custom-call(s32[1]{0:T(128)S(6)} %copy.19.s_shift, bf16[4,2,4,64,128]{4,3,2,1,0:T(8,128)(2,1)S(1)} %get-tuple-element.13.part, f32[8,128]{1,0:T(8,128)S(1)} %get-tuple-element.14.div, ...), custom_call_target="tpu_custom_call" | custom-call | tf_op jit(solution)/shard_map/fold/pallas_call | solution.py:602
  122.7 0.6 copy.21
  123.3 0.6 copy.22
  123.9 0.6 copy.23
Async XLA Ops:
  2.0 1.0 copy-start
  3.0 1.0 copy-start.1
  4.1 1.0 copy-start.2
  5.1 1.0 copy-start.3
  6.2 0.9 copy-start.4
  7.1 0.9 copy-start.5
  8.0 0.9 copy-start.6
  46.1 0.7 copy-start.7

commit v2 on v1

v2 whole, which is shorter than its diff:
```python
import functools
import math

import jax
import jax.numpy as jnp
from jax import lax
from jax.experimental import pallas as pl
from jax.experimental.pallas import tpu as pltpu
from jax.sharding import PartitionSpec as P

MESH = pl.DeviceIdType.MESH
NEG = -1e30
TOK = 128
NZ = 8
NY = 4
PAIRS = 6
VMEM_LIMIT = 60 * 1024 * 1024
SLOTS = NY * NZ
PIECE = 320
ROWS = 256
CHUNK = 256
SUB = 64
FLIGHT = 3
PART = 272
KEYS = SLOTS * TOK
F32 = jnp.float32
BF16 = jnp.bfloat16


def place():
    seq = lax.axis_index("seq")
    head = lax.axis_index("head")
    return seq, head, seq // NZ, seq % NZ, head // 2, head % 2


def greet(peers):
    barrier = pltpu.get_barrier_semaphore()
    for peer in peers:
        pl.semaphore_signal(barrier, inc=1, device_id=peer, device_id_type=MESH)
    return lambda: pl.semaphore_wait(barrier, len(peers))


def remote(src, dst, send, recv, device):
    return pltpu.make_async_remote_copy(
        src_ref=src, dst_ref=dst, send_sem=send, recv_sem=recv, device_id=device, device_id_type=MESH
    )


def spread_kernel(
    t_shift, s_shift, tq, tk, tv, hidden, wq, wk, wv,
    keys, cols,
    teach, tokens, weights, near_n, near_p, small_n, small_p, stud, piece, transit, hid,
    load, n_send, n_recv, p_send, p_recv,
    k_send, key_sem, tr_sem, f_send, g_send, r_send, z_send, z_recv, h_send, h_recv,
):
    seq, head, y, z, x, c = place()
    sibling = (seq, head + 1 - 2 * c)
    behind = (seq, (head + 7) % 8)
    teachers = (tq, tk, tv)
    loads = [pltpu.make_async_copy(hidden, tokens, load.at[0])]
    for kind, weight in enumerate((wq, wk, wv)):
        loads.append(pltpu.make_async_copy(weight, weights.at[kind], load.at[1 + kind]))
    for kind in range(3):
        loads.append(pltpu.make_async_copy(teachers[kind], teach.at[kind], load.at[4 + kind]))
    for copy in loads:
        copy.start()

    peers = [(seq, (head + d) % 8) for d in range(1, 8)]
    for dz in range(1, NZ):
        other = y * NZ + (z + dz) % NZ
        peers.append((other, head))
        peers.append((other, sibling[1]))
    for dy in range(1, NY):
        peers.append((((y + dy) % NY) * NZ + z, head))
    wait_all = greet(peers)

    loads[0].wait()
    for kind in range(3):
        loads[1 + kind].wait()
        stud[:, kind * 128 : (kind + 1) * 128] = jnp.dot(
            tokens[...], weights[kind], preferred_element_type=F32
        ).astype(BF16)
    wait_all()

    ahead = (seq, (head + 1) % 8)
    outs = []
    for kind in range(3):
        outs.append(remote(teachers[kind].at[:, 0:128], near_n.at[kind], n_send.at[kind], n_recv.at[kind], behind))
        outs.append(remote(teachers[kind].at[:, 384:512], near_p.at[kind], p_send.at[kind], p_recv.at[kind], ahead))
    outs.append(remote(stud, small_n, n_send.at[3], n_recv.at[3], behind))
    outs.append(remote(stud, small_p, p_send.at[3], p_recv.at[3], ahead))
    for copy in outs:
        copy.start()

    for part in range(4):
        first = pl.multiple_of(head // 2 * 512 + part * 128, 128)
        hid[part] = jnp.transpose(tokens[:, pl.ds(first, 128)].astype(F32)).astype(BF16)
    mine = pl.ds(pl.multiple_of(c * 64, 64), 64)
    column_outs = []
    for d in range(1, 4):
        to = (z + 2 * d) % NZ
        column_outs.append(
            remote(
                hid.at[to // 2, mine], cols.at[head, z // 2], z_send.at[d], z_recv.at[z // 2], (y * NZ + to, head)
            )
        )
    for copy in column_outs:
        copy.start()
    pltpu.make_async_copy(hid.at[z // 2, mine], cols.at[head, z // 2], z_recv.at[z // 2]).start()

    def one_hot(rows, columns, first, dim):
        there = lax.broadcasted_iota(jnp.int32, (rows, columns), dim)
        here = lax.broadcasted_iota(jnp.int32, (rows, columns), 1 - dim)
        return jnp.where(there == here + first, jnp.float32(1.0), jnp.float32(0.0)).astype(BF16)

    pick_t = one_hot(512, 256, t_shift[0] - 128, 0)
    pick_s = (one_hot(64, 256, s_shift[0] + 64, 1), one_hot(64, 256, s_shift[0], 1))
    own_pair = c == y // 2
    core = z % 2

    def send_piece(k, go):
        target = (y * NZ + k, 2 * x + core)
        some = k < PAIRS
        here = jnp.logical_and(some, jnp.logical_and(z == k, core == c))
        there = jnp.logical_and(some, jnp.logical_not(here))

        @pl.when(jnp.logical_and(own_pair, there))
        def _():
            copy = remote(piece.at[k], keys.at[seq], k_send.at[k], key_sem.at[seq], target)
            copy.start() if go else copy.wait_send()

        @pl.when(jnp.logical_and(jnp.logical_not(own_pair), there))
        def _():
            copy = remote(piece.at[k], transit.at[z // 2], k_send.at[k], tr_sem.at[z // 2], target)
            copy.start() if go else copy.wait_send()

        if go:
            @pl.when(jnp.logical_and(own_pair, here))
            def _():
                pltpu.make_async_copy(piece.at[k], keys.at[seq], key_sem.at[seq]).start()

            @pl.when(jnp.logical_and(jnp.logical_not(own_pair), here))
            def _():
                pltpu.make_async_copy(piece.at[k], transit.at[z // 2], tr_sem.at[z // 2]).start()

    transposed = (((1,), (1,)), ((), ()))
    for copy in loads[4:]:
        copy.wait()
    for copy in outs[6:]:
        copy.wait_recv()
    for kind in range(3):
        outs[2 * kind].wait_recv()
        outs[2 * kind + 1].wait_recv()
        at = slice(kind * 128, (kind + 1) * 128)
        for j in range(2):
            own = teach[kind, :, 0:384] if j == 0 else teach[kind, :, 128:512]
            if j == 0:
                window = jnp.dot(near_p[kind], pick_t[0:128], preferred_element_type=F32) + jnp.dot(
                    own, pick_t[128:512], preferred_element_type=F32
                )
                before, after = small_p[:, at], stud[:, at]
            else:
                window = jnp.dot(own, pick_t[0:384], preferred_element_type=F32) + jnp.dot(
                    near_n[kind], pick_t[384:512], preferred_element_type=F32
                )
                before, after = stud[:, at], small_n[:, at]
            small = lax.dot_general(
                pick_s[j][:, 0:128], before, transposed, preferred_element_type=F32
            ) + lax.dot_general(pick_s[j][:, 128:256], after, transposed, preferred_element_type=F32)
            k = kind * 2 + j
            piece[k, 0:128] = window[:, 0:128].astype(BF16)
            piece[k, 128:256] = window[:, 128:256].astype(BF16)
            piece[k, 256:320] = small.astype(BF16)
    order = [(z + d + NZ) % NZ for d in (0, 1, -1, 2, -2, 3, -3, 4)]
    for n, k in enumerate(order):
        if n > FLIGHT:
            send_piece(order[n - 1 - FLIGHT], False)
        send_piece(k, True)

    active = z < PAIRS

    def key_copy(slot, send, device):
        return remote(keys.at[slot], keys.at[slot], send, key_sem.at[slot], device)

    partner = ((y + 1 - 2 * (y % 2)) * NZ + z, head)
    far_row = 2 * (1 - y // 2)

    def forwards(i):
        slot = y * NZ + 2 * i + c
        first = key_copy(slot, f_send.at[i], partner)
        relay = key_copy(slot, r_send.at[i], sibling)
        others = [
            remote(transit.at[i], keys.at[slot], g_send.at[2 * i + b], key_sem.at[slot], ((far_row + b) * NZ + z, head))
            for b in range(2)
        ]
        return first, relay, others

    def arrival(turn):
        same = (0, 2, 6, 4)[turn]
        cross = (1, 7, 3, 5)[turn]
        return (z + jnp.where(core == c, same, cross)) % NZ // 2

    @pl.when(active)
    def _():
        for turn in range(4):
            i = arrival(turn)
            first, relay, others = forwards(i)
            remote(transit.at[i], transit.at[i], g_send.at[2 * i], tr_sem.at[i], partner).wait_recv()
            for copy in others:
                copy.start()
            first.wait_recv()
            first.start()
            relay.start()

    for i in range(4):
        pltpu.make_async_copy(hid.at[i, mine], cols.at[head, i], z_recv.at[i]).wait()
    head_outs = []
    for d in range(1, 8):
        head_outs.append(
            remote(cols.at[head], cols.at[head], h_send.at[d], h_recv.at[head], (seq, (head + d) % 8))
        )
    for copy in head_outs:
        copy.start()

    @pl.when(active)
    def _():
        for turn in range(4):
            i = arrival(turn)
            for n in range(3):
                other = y // 2 * 2 + 1 - y % 2 if n == 0 else far_row + n - 1
                slot = other * NZ + 2 * i + c
                relay = key_copy(slot, r_send.at[4 + 3 * turn + n], sibling)
                relay.wait_recv()
                relay.start()
        for i in range(4):
            for row in range(NY):
                slot = row * NZ + 2 * i + 1 - c
                key_copy(slot, r_send.at[0], sibling).wait_recv()
        for i in range(4):
            first, relay, others = forwards(i)
            first.wait_send()
            relay.wait_send()
            for copy in others:
                copy.wait_send()
            for n in range(3):
                key_copy(0, r_send.at[4 + 3 * i + n], sibling).wait_send()

    for d in range(1, 8):
        other = (head + d) % 8
        remote(cols.at[other], cols.at[other], h_send.at[d], h_recv.at[other], sibling).wait_recv()
    for copy in head_outs + column_outs + outs:
        copy.wait_send()
    for k in order[NZ - 1 - FLIGHT :]:
        send_piece(k, False)


def spread(t_shift, s_shift, tq, tk, tv, hidden, wq, wk, wv):
    anywhere = pl.BlockSpec(memory_space=pl.ANY)
    smem = pl.BlockSpec(memory_space=pltpu.SMEM)
    dma = pltpu.SemaphoreType.DMA
    return pl.pallas_call(
        spread_kernel,
        name="spread",
        out_shape=(
            jax.ShapeDtypeStruct((SLOTS, PIECE, 128), BF16),
            jax.ShapeDtypeStruct((8, 4, 64, TOK), BF16),
        ),
        in_specs=[smem, smem] + [anywhere] * 7,
        out_specs=(anywhere, anywhere),
        scratch_shapes=[
            pltpu.VMEM((3, TOK, 512), BF16),
            pltpu.VMEM((TOK, 2048), BF16),
            pltpu.VMEM((3, 2048, 128), BF16),
            pltpu.VMEM((3, TOK, 128), BF16),
            pltpu.VMEM((3, TOK, 128), BF16),
            pltpu.VMEM((TOK, 384), BF16),
            pltpu.VMEM((TOK, 384), BF16),
            pltpu.VMEM((TOK, 384), BF16),
            pltpu.VMEM((NZ, PIECE, 128), BF16),
            pltpu.VMEM((4, PIECE, 128), BF16),
            pltpu.VMEM((4, 128, TOK), BF16),
            dma((7,)), dma((4,)), dma((4,)), dma((4,)), dma((4,)),
            dma((NZ,)), dma((SLOTS,)), dma((4,)), dma((4,)), dma((8,)), dma((16,)),
            dma((4,)), dma((4,)), dma((8,)), dma((8,)),
        ],
        compiler_params=pltpu.CompilerParams(
            collective_id=0, has_side_effects=True, vmem_limit_bytes=VMEM_LIMIT
        ),
    )(t_shift, s_shift, tq, tk, tv, hidden, wq, wk, wv)


def in_three(row):
    high = row.astype(BF16).astype(F32)
    middle = (row - high).astype(BF16).astype(F32)
    low = row - high - middle
    at = lax.broadcasted_iota(jnp.int32, (16, 128), 0)
    tile = jnp.where(at == 0, high, jnp.where(at == 1, middle, jnp.where(at == 2, low, jnp.float32(0.0))))
    return tile.astype(BF16)


def relate_kernel(
    lengths, keys, part, div, kt, kst, st, ss, acc, top_t, top_s, row_t, row_s, cross, begin, load
):
    _, _, y, z, _, c = place()
    group = 2 * (y % 2) + c
    div[...] = jnp.zeros_like(div)
    coef = jnp.float32(1.0 / 48.0)
    scale = jnp.float32(1.0 / 16.0)
    scale2 = jnp.float32(math.log2(math.e) / 16.0)
    span = CHUNK // TOK
    blocks = KEYS // ROWS

    @pl.when(z < PAIRS)
    def _():
        loads = [
            pltpu.make_async_copy(keys.at[:, 0:128], kt.at[:, :, 0:128], load.at[0]),
            pltpu.make_async_copy(keys.at[:, 128:256], kt.at[:, :, 128:256], load.at[1]),
            pltpu.make_async_copy(keys.at[:, 256:320], kst, load.at[2]),
        ]
        for copy in loads:
            copy.start()
        acc[...] = jnp.zeros_like(acc)
        end0 = lengths[0]
        end1 = end0 + lengths[1]
        end2 = end1 + lengths[2]

        def first_of(position):
            zero = jnp.int32(0)
            start = jnp.where(position >= end0, end0, zero)
            start = jnp.where(position >= end1, end1, start)
            return jnp.where(position >= end2, end2, start)

        most = jnp.maximum(jnp.maximum(lengths[0], lengths[1]), jnp.maximum(lengths[2], lengths[3]))
        last = jnp.where(
            lengths[0] == most, end0, jnp.where(lengths[1] == most, end1, jnp.where(lengths[2] == most, end2, KEYS))
        )
        last_block = (last - 1) // ROWS
        for copy in loads:
            copy.wait()

        @pl.loop(0, 4)
        def _(t):
            odd = t % 2
            nth = 4 * t + odd * 3 + (1 - 2 * odd) * group
            block = (last_block + blocks - nth) % blocks
            r0 = block * ROWS
            lower = first_of(r0) // CHUNK
            upper = (r0 + ROWS - 1) // CHUNK + 1
            latest = first_of(r0 + ROWS - 1)
            top_t[...] = jnp.full_like(top_t, NEG)
            top_s[...] = jnp.full_like(top_s, NEG)
            begin[...] = first_of(r0 + lax.broadcasted_iota(jnp.int32, (ROWS, 128), 0))
            two = ROWS // TOK
            bt = jnp.concatenate([kst[block * two + u] for u in range(two)], axis=1)
            b2 = (jnp.transpose(bt.astype(F32)) * jnp.float32(2.0)).astype(BF16)

            def key_columns(n):
                return jnp.concatenate([kst[n * span + u] for u in range(span)], axis=1)

            def scores(n):
                a = lax.dot_general(
                    kt[pl.ds(block * two, two)].reshape(ROWS, 256),
                    kt[pl.ds(n * span, span)].reshape(CHUNK, 256),
                    (((1,), (1,)), ((), ())),
                    preferred_element_type=F32,
                )
                return a, jnp.dot(b2, key_columns(n), preferred_element_type=F32)

            def online(n, a, b, allowed):
                k0 = pl.multiple_of(n * CHUNK, CHUNK)
                for r in range(0, ROWS, SUB):
                    rows = slice(r, r + SUB)
                    xs = []
                    ws = []
                    for q in range(span):
                        x = a[rows, q * 128 : q * 128 + 128]
                        w = b[rows, q * 128 : q * 128 + 128]
                        if allowed is not None:
                            keep = allowed(k0 + q * 128, r)
                            x = jnp.where(keep, x, NEG)
                            w = jnp.where(keep, w, NEG)
                        at = pl.ds(pl.multiple_of(k0 + q * 128, 128), 128)
                        st[rows, at] = x
                        ss[rows, at] = w
                        xs.append(x)
                        ws.append(w)
                    old_t = top_t[rows]
                    old_s = top_s[rows]
                    mt = functools.reduce(jnp.maximum, xs, old_t)
                    ms = functools.reduce(jnp.maximum, ws, old_s)
                    top_t[rows] = mt
                    top_s[rows] = ms
                    fade = jnp.exp2((old_t - mt) * scale2)
                    tot_t = row_t[rows] * fade
                    mix = cross[rows] * fade
                    tot_s = row_s[rows] * jnp.exp2((old_s - ms) * scale2)
                    for x, w in zip(xs, ws):
                        ea = jnp.exp2((x - mt) * scale2)
                        tot_t = tot_t + ea
                        tot_s = tot_s + jnp.exp2((w - ms) * scale2)
                        mix = mix + ea * (x - w)
                    row_t[rows] = tot_t
                    row_s[rows] = tot_s
                    cross[rows] = mix

            def masked(n):
                def allowed(c0, r):
                    row = r0 + r + lax.broadcasted_iota(jnp.int32, (SUB, 128), 0)
                    column = c0 + lax.broadcasted_iota(jnp.int32, (SUB, 128), 1)
                    return jnp.logical_and(column >= begin[r : r + SUB], column <= row)

                online(n, *scores(n), allowed)

            def whole(n):
                online(n, *scores(n), None)

            row_t[...] = jnp.zeros_like(row_t)
            row_s[...] = jnp.zeros_like(row_s)
            cross[...] = jnp.zeros_like(cross)
            inner = jnp.minimum((latest + CHUNK - 1) // CHUNK, upper)
            outer = jnp.maximum((r0 + 1) // CHUNK, inner)

            @pl.loop(0, upper - lower - (outer - inner))
            def _(n):
                masked(jnp.where(lower + n < inner, lower + n, lower + n + (outer - inner)))

            @pl.loop(inner, outer)
            def _(n):
                whole(n)

            mt = jnp.max(top_t[...], axis=1, keepdims=True)
            ms = jnp.max(top_s[...], axis=1, keepdims=True)
            fade = jnp.exp2((top_t[...] - mt) * scale2)
            tot_t = jnp.sum(row_t[...] * fade, axis=1, keepdims=True)
            tot_s = jnp.sum(row_s[...] * jnp.exp2((top_s[...] - ms) * scale2), axis=1, keepdims=True)
            mixed = jnp.sum(cross[...] * fade, axis=1, keepdims=True)
            value = (mixed / tot_t + (ms - mt)) * scale + (jnp.log(tot_s) - jnp.log(tot_t))
            wide = jnp.broadcast_to(value * jnp.float32(1.0 / 128.0), (ROWS, 128))
            div[...] += jnp.sum(wide.reshape(ROWS // 8, 8, 128), axis=0)
            top_t[...] = jnp.broadcast_to(mt, (ROWS, 128))
            top_s[...] = jnp.broadcast_to(ms, (ROWS, 128))
            row_t[...] = jnp.broadcast_to(jnp.log2(coef / tot_t), (ROWS, 128))
            row_s[...] = jnp.broadcast_to(jnp.log2(coef / tot_s), (ROWS, 128))

            def gradient(n, near):
                k0 = pl.multiple_of(n * CHUNK, CHUNK)
                columns = []
                for q in range(span):
                    at = pl.ds(pl.multiple_of(k0 + q * 128, 128), 128)
                    columns.append(
                        (
                            jnp.exp2((ss[:, at] - top_s[...]) * scale2 + row_s[...])
                            - jnp.exp2((st[:, at] - top_t[...]) * scale2 + row_t[...])
                        ).astype(BF16)
                    )
                g = jnp.concatenate(columns, axis=1)
                acc[:, pl.ds(k0, CHUNK)] += jnp.dot(bt, g, preferred_element_type=F32)
                return near + lax.dot_general(
                    key_columns(n), g, (((1,), (1,)), ((), ())), preferred_element_type=F32
                )

            near = lax.fori_loop(lower, upper, gradient, jnp.zeros((64, ROWS), F32))
            acc[:, pl.ds(pl.multiple_of(r0, ROWS), ROWS)] += near

        tile = in_three(jnp.sum(div[...], axis=0, keepdims=True))
        for row in range(NY):
            for parity in range(2):
                for i in range(4):
                    base = (row * NZ + 2 * i + parity) * TOK
                    part[row, parity, i * 64 : (i + 1) * 64] = (
                        acc[:, base : base + TOK] * jnp.float32(1.0 / 8.0)
                    ).astype(BF16)
                part[row, parity, 256:PART] = tile


def relate(lengths, keys):
    vmem = pl.BlockSpec(memory_space=pltpu.VMEM)
    smem = pl.BlockSpec(memory_space=pltpu.SMEM)
    return pl.pallas_call(
        relate_kernel,
        name="relate",
        out_shape=(
            jax.ShapeDtypeStruct((NY, 2, PART, 128), BF16)
        ),
        in_specs=[smem, pl.BlockSpec(memory_space=pl.ANY)],
        out_specs=vmem,
        scratch_shapes=[
            pltpu.VMEM((8, 128), F32),
            pltpu.VMEM((SLOTS, TOK, 256), BF16),
            pltpu.VMEM((SLOTS, 64, TOK), BF16),
            pltpu.VMEM((ROWS, KEYS), F32),
            pltpu.VMEM((ROWS, KEYS), F32),
            pltpu.VMEM((64, KEYS), F32),
            pltpu.VMEM((ROWS, 128), F32),
            pltpu.VMEM((ROWS, 128), F32),
            pltpu.VMEM((ROWS, 128), F32),
            pltpu.VMEM((ROWS, 128), F32),
            pltpu.VMEM((ROWS, 128), F32),
            pltpu.VMEM((ROWS, 128), jnp.int32),
            pltpu.SemaphoreType.DMA((3,)),
        ],
        compiler_params=pltpu.CompilerParams(vmem_limit_bytes=VMEM_LIMIT),
    )(lengths, keys)


def fold_kernel(
    part, cols, mean, both,
    in1, sums, in2, outp, in4, win, prev, follow, div_x, div_1, fetched,
    load, s1, r1, s2, r2, s4, r4, sw, rw, sv, rv, sx, rx,
):
    seq, head, y, z, x, c = place()
    ahead = (seq, (head + 1) % 8)
    behind = (seq, (head + 7) % 8)
    other = head + 1 - 2 * c
    fetch = pltpu.make_async_copy(cols, fetched, load)
    fetch.start()
    peers = [(seq, (head + d) % 8) for d in range(1, 8)]
    for dz in range(1, NZ):
        for h in (head, other):
            peers.append((y * NZ + (z + dz) % NZ, h))
    for dy in range(1, NY):
        for h in (head, other):
            peers.append((((y + dy) % NY) * NZ + z, h))
        peers.append((((y + dy) % NY) * NZ + z + 1 - 2 * (z % 2), head))
    greet(peers)()
    active = z < PAIRS

    def row_copies():
        me = y * 2 + c
        copies = []
        for dy in (2, 1, 3):
            row = (y + dy) % NY
            for core in range(2):
                copies.append(
                    remote(part.at[row, core], in1.at[me], s1.at[2 * dy + core], r1.at[me], (row * NZ + z, 2 * x + core))
                )
        copies.append(remote(part.at[y, 1 - c], in1.at[me], s1.at[0], r1.at[me], (seq, other)))
        return copies

    @pl.when(active)
    def _():
        for copy in row_copies():
            copy.start()
        pltpu.make_async_copy(part.at[y, c], in1.at[y * 2 + c], r1.at[y * 2 + c]).start()

    def each_pair_copy(p, go):
        for i in range(4):
            copy = remote(sums.at[p], in2.at[z], s2.at[p * 4 + i], r2.at[z], (y * NZ + 2 * i + c, 2 * x + p))
            mine = jnp.logical_and(z == 2 * i + c, c == p)

            @pl.when(jnp.logical_not(mine))
            def _():
                copy.start() if go else copy.wait_send()

            if go:
                @pl.when(mine)
                def _():
                    pltpu.make_async_copy(sums.at[p], in2.at[z], r2.at[z]).start()

    @pl.when(active)
    def _():
        for p in range(2):
            total = jnp.zeros((256, 128), F32)
            tiles = jnp.zeros((16, 128), F32)
            for n in range(4 * p, 4 * p + 4):
                pltpu.make_async_copy(in1.at[n], in1.at[n], r1.at[n]).wait()
                total = total + in1[n, 0:256].astype(F32)
                tiles = tiles + in1[n, 256:PART].astype(F32)
            sums[p, 0:256] = total.astype(BF16)
            sums[p, 256:PART] = in_three(jnp.sum(tiles, axis=0, keepdims=True))
            each_pair_copy(p, True)

    fetch.wait()
    tiles = jnp.zeros((16, 128), F32)
    for k in range(PAIRS):
        pltpu.make_async_copy(in2.at[k], in2.at[k], r2.at[k]).wait()
        tiles = tiles + in2[k, 256:PART].astype(F32)
    grad = jnp.zeros((512, 384), F32)
    for i in range(4):
        grad = grad + lax.dot_general(
            fetched[:, i].reshape(512, TOK), in2[:, i * 64 : (i + 1) * 64].reshape(384, TOK),
            (((1,), (1,)), ((), ())),
            preferred_element_type=F32,
        )
    for n in range(8):
        outp[n] = grad[n * 64 : (n + 1) * 64].astype(BF16)

    slot = y * 2 + z % 2
    block_copies = []
    for d in (4, 5, 2, 3, 6, 7, 1):
        to = (slot + d) % 8
        block_copies.append(
            remote(
                outp.at[to], in4.at[slot], s4.at[d], r4.at[slot],
                ((to // 2) * NZ + (z // 2) * 2 + to % 2, head),
            )
        )
    for copy in block_copies:
        copy.start()
    pltpu.make_async_copy(outp.at[slot], in4.at[slot], r4.at[slot]).start()

    div_1[...] = jnp.broadcast_to(jnp.sum(tiles, axis=0, keepdims=True), (8, 128))
    pltpu.make_async_copy(div_1, div_x.at[head], rx.at[head]).start()
    div_copies = [remote(div_1, div_x.at[head], sx.at[d], rx.at[head], (seq, (head + d) % 8)) for d in range(1, 8)]
    for copy in div_copies:
        copy.start()

    total = jnp.zeros((64, 384), F32)
    for n in range(8):
        pltpu.make_async_copy(in4.at[n], in4.at[n], r4.at[n]).wait()
        total = total + in4[n].astype(F32)
    win[...] = total.astype(BF16)
    lasts = [remote(win, prev, sw, rw, ahead), remote(win, follow, sv, rv, behind)]
    for copy in lasts:
        copy.start()
    both[:, 384:768] = win[...]
    for copy in block_copies + div_copies:
        copy.wait_send()

    @pl.when(active)
    def _():
        for copy in row_copies():
            copy.wait_send()
        for p in range(2):
            each_pair_copy(p, False)

    total = jnp.zeros((8, 128), F32)
    for n in range(8):
        pltpu.make_async_copy(div_x.at[n], div_x.at[n], rx.at[n]).wait()
        total = total + div_x[n]
    mean[0, 0] = jnp.sum(total[0:1]) * jnp.float32(1.0 / 196608.0)
    for copy in lasts:
        copy.wait_send()
        copy.wait_recv()
    both[:, 0:384] = prev[...]
    both[:, 768:1152] = follow[...]


def fold(part, cols):
    vmem = pl.BlockSpec(memory_space=pltpu.VMEM)
    smem = pl.BlockSpec(memory_space=pltpu.SMEM)
    dma = pltpu.SemaphoreType.DMA
    return pl.pallas_call(
        fold_kernel,
        name="fold",
        out_shape=(jax.ShapeDtypeStruct((1, 1), F32), jax.ShapeDtypeStruct((64, 1152), BF16)),
        in_specs=[pl.BlockSpec(memory_space=pl.ANY)] * 2,
        out_specs=(smem, vmem),
        scratch_shapes=[
            pltpu.VMEM((8, PART, 128), BF16),
            pltpu.VMEM((2, PART, 128), BF16),
            pltpu.VMEM((PAIRS, PART, 128), BF16),
            pltpu.VMEM((8, 64, 384), BF16),
            pltpu.VMEM((8, 64, 384), BF16),
            pltpu.VMEM((64, 384), BF16),
            pltpu.VMEM((64, 384), BF16),
            pltpu.VMEM((64, 384), BF16),
            pltpu.VMEM((8, 8, 128), F32),
            pltpu.VMEM((8, 128), F32),
            pltpu.VMEM((8, 4, 64, TOK), BF16),
            dma(()), dma((8,)), dma((8,)), dma((8,)), dma((PAIRS,)), dma((8,)), dma((8,)),
            dma(()), dma(()), dma(()), dma(()), dma((8,)), dma((8,)),
        ],
        compiler_params=pltpu.CompilerParams(
            collective_id=1, has_side_effects=True, vmem_limit_bytes=VMEM_LIMIT
        ),
    )(part, cols)


def shift_kernel(s_shift, both, gq, gk, gv):
    there = lax.broadcasted_iota(jnp.int32, (384, 128), 0)
    here = lax.broadcasted_iota(jnp.int32, (384, 128), 1)
    pick = jnp.where(there == here + (192 - s_shift[0]), jnp.float32(1.0), jnp.float32(0.0)).astype(BF16)
    for kind, out in enumerate((gq, gk, gv)):
        out[...] = functools.reduce(
            jnp.add,
            [
                jnp.dot(
                    both[:, 384 * n + 128 * kind : 384 * n + 128 * kind + 128],
                    pick[128 * n : 128 * n + 128],
                    preferred_element_type=F32,
                )
                for n in range(3)
            ],
        ).astype(BF16)


def shift(s_shift, both):
    vmem = pl.BlockSpec(memory_space=pltpu.VMEM)
    grad = jax.ShapeDtypeStruct((64, 128), BF16)
    return pl.pallas_call(
        shift_kernel,
        name="shift",
        out_shape=(grad, grad, grad),
        in_specs=[pl.BlockSpec(memory_space=pltpu.SMEM), vmem],
        out_specs=(vmem, vmem, vmem),
    )(s_shift, both)


def local(
    teacher_query, teacher_key, teacher_value, student_hidden, weight_query, weight_key, weight_value,
    teacher_shift, student_shift, segment_lengths,
):
    keys, cols = spread(
        teacher_shift, student_shift, teacher_query, teacher_key, teacher_value, student_hidden,
        weight_query, weight_key, weight_value,
    )
    mean, both = fold(relate(segment_lengths, keys), cols)
    return (mean[0, 0], *shift(student_shift, both))


def solution(mesh):
    in_specs = (
        P("seq", "head"),
        P("seq", "head"),
        P("seq", "head"),
        P("seq", None),
        P(None, "head"),
        P(None, "head"),
        P(None, "head"),
        P(),
        P(),
        P(),
    )
    out_specs = (P(), P("seq", "head"), P("seq", "head"), P("seq", "head"))
    return jax.shard_map(local, mesh=mesh, in_specs=in_specs, out_specs=out_specs, check_vma=False)
```

time: 126 us -> 99.1 us (0.79)
  Pallas kernels: 112 us -> 95.2 us
  local copies, waits for them, and re-layouts: 9.34 us -> 0 us
    pallas_call x1 -> x2, Pallas kernels: 29.8 us -> 18.9 us  [the longest x1 17.2 us: relate(): pl.pallas_call(relate_kernel, name='relate', out_shape=jax.ShapeDtypeStru...]
    pallas_call x1, Pallas kernels: 45.5 us -> 36.1 us  [fold(): pl.pallas_call(fold_kernel, name='fold', out_shape=(jax.ShapeDtypeStruct(...]
    unnamed x19 -> x0, local copies, waits for them, and re-layouts: 9.34 us -> none
    pallas_call x1, Pallas kernels: 37.2 us -> 40.2 us  [spread(): pl.pallas_call(spread_kernel, name='spread', out_shape=(jax.ShapeDtypeStr...]
where the time goes in v2:
time: 99.1 us; the launch traced here: 98.9 us
  Pallas kernels  95.2 us (96%)
  between operations  3.7 us (4%)
    pallas_call x1, Pallas kernels, spread(): pl.pallas_call(spread_kernel, name='spread', out_shape=(jax.ShapeDtypeStr...  40.2 us
    pallas_call x1, Pallas kernels, fold(): pl.pallas_call(fold_kernel, name='fold', out_shape=(jax.ShapeDtypeStruct(...  36.1 us
    pallas_call x1, Pallas kernels, relate(): pl.pallas_call(relate_kernel, name='relate', out_shape=jax.ShapeDtypeStru...  17.2 us

profile of v2, /device:TPU:1, one launch (start us, length us, event | category | flops | bytes accessed | tf_op | source)
XLA Modules:
  0.0 98.9 jit_solution(7992003712220775602)
XLA Ops:
  1.9 40.2 %spread.1 = (bf16[32,320,128]{2,1,0:T(8,128)(2,1)}, bf16[8,4,64,128]{3,2,1,0:T(8,128)(2,1)}) custom-call(s32[1]{0:T(128)S(6)} %copy.15.t_shift, s32[1]{0:T(128)S(6)} %copy.16.s_shift, bf16[128,512]{1,0:T(8,128)(2,1)} %tq.1, bf16[128,512]{1,0:T(8,128)(2,1)} %tk.1, bf16[128,512]{1,0:T(8,128)(2,1)} %tv.1, bf16[128,2048]{1,0:T(8,128)(2,1)} %hidden.1, ...), custom_call_target="tpu_custom_call" | custom-call | tf_op jit(solution)/shard_map/spread/pallas_call | solution.py:261
  42.1 17.2 %relate.1.part = bf16[4,2,272,128]{3,2,1,0:T(8,128)(2,1)} custom-call(s32[4]{0:T(128)} %lengths.1, bf16[32,320,128]{2,1,0:T(8,128)(2,1)} %get-tuple-element.11.keys), custom_call_target="tpu_custom_call" | custom-call | tf_op jit(solution)/shard_map/relate/pallas_call | solution.py:479
  59.3 36.1 %fold.1 = (f32[1,1]{1,0:T(1,128)}, bf16[64,1152]{1,0:T(8,128)(2,1)}) custom-call(bf16[4,2,272,128]{3,2,1,0:T(8,128)(2,1)} %relate.1.part, bf16[8,4,64,128]{3,2,1,0:T(8,128)(2,1)} %get-tuple-element.12.cols), custom_call_target="tpu_custom_call" | custom-call | tf_op jit(solution)/shard_map/fold/pallas_call | solution.py:643
  95.4 1.7 %shift.1 = (bf16[64,128]{1,0:T(8,128)(2,1)}, bf16[64,128]{1,0:T(8,128)(2,1)}, bf16[64,128]{1,0:T(8,128)(2,1)}) custom-call(s32[1]{0:T(128)S(6)} %copy.16.s_shift, bf16[64,1152]{1,0:T(8,128)(2,1)} %get-tuple-element.14.both), custom_call_target="tpu_custom_call" | custom-call | tf_op jit(solution)/shard_map/shift/pallas_call | solution.py:691

commit v3 on v2

--- a/solution.py
+++ b/solution.py
@@ -18,9 +18,8 @@
 SLOTS = NY * NZ
 PIECE = 320
 ROWS = 256
-CHUNK = 256
-SUB = 64
-FLIGHT = 3
+CHUNK = 512
+FLIGHT = 2
 PART = 272
 KEYS = SLOTS * TOK
 F32 = jnp.float32
@@ -31,6 +30,10 @@
     seq = lax.axis_index("seq")
     head = lax.axis_index("head")
     return seq, head, seq // NZ, seq % NZ, head // 2, head % 2
+
+
+def pair_at(z, group):
+    return (z + 4 * group) % NZ
 
 
 def greet(peers):
@@ -49,7 +52,7 @@
 def spread_kernel(
     t_shift, s_shift, tq, tk, tv, hidden, wq, wk, wv,
     keys, cols,
-    teach, tokens, weights, near_n, near_p, small_n, small_p, stud, piece, transit, hid,
+    stack, tokens, weights, small_n, small_p, stud, piece, transit, hid,
     load, n_send, n_recv, p_send, p_recv,
     k_send, key_sem, tr_sem, f_send, g_send, r_send, z_send, z_recv, h_send, h_recv,
 ):
@@ -61,7 +64,14 @@
     for kind, weight in enumerate((wq, wk, wv)):
         loads.append(pltpu.make_async_copy(weight, weights.at[kind], load.at[1 + kind]))
     for kind in range(3):
-        loads.append(pltpu.make_async_copy(teachers[kind], teach.at[kind], load.at[4 + kind]))
+        for j in range(2):
+            loads.append(
+                pltpu.make_async_copy(
+                    teachers[kind].at[:, 128 * j : 128 * j + 384],
+                    stack.at[2 * kind + j, :, 128 - 128 * j : 512 - 128 * j],
+                    load.at[4 + 2 * kind + j],
+                )
+            )
     for copy in loads:
         copy.start()
 
@@ -85,8 +95,11 @@
     ahead = (seq, (head + 1) % 8)
     outs = []
     for kind in range(3):
-        outs.append(remote(teachers[kind].at[:, 0:128], near_n.at[kind], n_send.at[kind], n_recv.at[kind], behind))
-        outs.append(remote(teachers[kind].at[:, 384:512], near_p.at[kind], p_send.at[kind], p_recv.at[kind], ahead))
+        first, last = teachers[kind].at[:, 0:128], teachers[kind].at[:, 384:512]
+        outs.append(
+            remote(first, stack.at[2 * kind + 1, :, 384:512], n_send.at[kind], n_recv.at[kind], behind)
+        )
+        outs.append(remote(last, stack.at[2 * kind, :, 0:128], p_send.at[kind], p_recv.at[kind], ahead))
     outs.append(remote(stud, small_n, n_send.at[3], n_recv.at[3], behind))
     outs.append(remote(stud, small_p, p_send.at[3], p_recv.at[3], ahead))
     for copy in outs:
@@ -118,10 +131,11 @@
     own_pair = c == y // 2
     core = z % 2
 
-    def send_piece(k, go):
-        target = (y * NZ + k, 2 * x + core)
+    def send_piece(to, go):
+        k = pair_at(to, c)
+        target = (y * NZ + to, 2 * x + core)
         some = k < PAIRS
-        here = jnp.logical_and(some, jnp.logical_and(z == k, core == c))
+        here = jnp.logical_and(some, jnp.logical_and(z == to, core == c))
         there = jnp.logical_and(some, jnp.logical_not(here))
 
         @pl.when(jnp.logical_and(own_pair, there))
@@ -146,68 +160,68 @@
     transposed = (((1,), (1,)), ((), ()))
     for copy in loads[4:]:
         copy.wait()
+    for copy in outs[:6]:
+        copy.wait_recv()
+    window = jnp.dot(stack[...].reshape(PAIRS * TOK, 512), pick_t, preferred_element_type=F32)
+    for k in range(PAIRS):
+        piece[k, 0:128] = window[k * TOK : (k + 1) * TOK, 0:128].astype(BF16)
+        piece[k, 128:256] = window[k * TOK : (k + 1) * TOK, 128:256].astype(BF16)
     for copy in outs[6:]:
         copy.wait_recv()
-    for kind in range(3):
-        outs[2 * kind].wait_recv()
-        outs[2 * kind + 1].wait_recv()
-        at = slice(kind * 128, (kind + 1) * 128)
-        for j in range(2):
-            own = teach[kind, :, 0:384] if j == 0 else teach[kind, :, 128:512]
-            if j == 0:
-                window = jnp.dot(near_p[kind], pick_t[0:128], preferred_element_type=F32) + jnp.dot(
-                    own, pick_t[128:512], preferred_element_type=F32
-                )
-                before, after = small_p[:, at], stud[:, at]
-            else:
-                window = jnp.dot(own, pick_t[0:384], preferred_element_type=F32) + jnp.dot(
-                    near_n[kind], pick_t[384:512], preferred_element_type=F32
-                )
-                before, after = stud[:, at], small_n[:, at]
-            small = lax.dot_general(
-                pick_s[j][:, 0:128], before, transposed, preferred_element_type=F32
-            ) + lax.dot_general(pick_s[j][:, 128:256], after, transposed, preferred_element_type=F32)
-            k = kind * 2 + j
-            piece[k, 0:128] = window[:, 0:128].astype(BF16)
-            piece[k, 128:256] = window[:, 128:256].astype(BF16)
-            piece[k, 256:320] = small.astype(BF16)
+    for k in range(PAIRS):
+        at = slice(k // 2 * 128, (k // 2 + 1) * 128)
+        before, after = (small_p, stud) if k % 2 == 0 else (stud, small_n)
+        pick = pick_s[k % 2]
+        small = lax.dot_general(
+            pick[:, 0:128], before[:, at], transposed, preferred_element_type=F32
+        ) + lax.dot_general(pick[:, 128:256], after[:, at], transposed, preferred_element_type=F32)
+        piece[k, 256:320] = small.astype(BF16)
     order = [(z + d + NZ) % NZ for d in (0, 1, -1, 2, -2, 3, -3, 4)]
-    for n, k in enumerate(order):
+    for n, to in enumerate(order):
         if n > FLIGHT:
             send_piece(order[n - 1 - FLIGHT], False)
-        send_piece(k, True)
-
-    active = z < PAIRS
+        send_piece(to, True)
+
+    active = pair_at(z, y // 2) < PAIRS
+    passing = pair_at(z, 1 - y // 2) < PAIRS
+    beside = y + 1 - 2 * (y % 2)
+    partner = (beside * NZ + z, head)
+    opposite = ((3 - y) * NZ + z, head)
 
     def key_copy(slot, send, device):
         return remote(keys.at[slot], keys.at[slot], send, key_sem.at[slot], device)
 
-    partner = ((y + 1 - 2 * (y % 2)) * NZ + z, head)
-    far_row = 2 * (1 - y // 2)
-
-    def forwards(i):
-        slot = y * NZ + 2 * i + c
-        first = key_copy(slot, f_send.at[i], partner)
-        relay = key_copy(slot, r_send.at[i], sibling)
-        others = [
-            remote(transit.at[i], keys.at[slot], g_send.at[2 * i + b], key_sem.at[slot], ((far_row + b) * NZ + z, head))
-            for b in range(2)
-        ]
-        return first, relay, others
-
-    def arrival(turn):
+    def source(turn):
         same = (0, 2, 6, 4)[turn]
         cross = (1, 7, 3, 5)[turn]
-        return (z + jnp.where(core == c, same, cross)) % NZ // 2
-
-    @pl.when(active)
-    def _():
-        for turn in range(4):
-            i = arrival(turn)
-            first, relay, others = forwards(i)
-            remote(transit.at[i], transit.at[i], g_send.at[2 * i], tr_sem.at[i], partner).wait_recv()
-            for copy in others:
+        return (z + jnp.where(core == c, same, cross)) % NZ
+
+    def forwards(turn):
+        slot = y * NZ + source(turn)
+        return key_copy(slot, f_send.at[turn], partner), key_copy(slot, r_send.at[turn], sibling)
+
+    def passed(turn):
+        slot = y * NZ + source(turn)
+        i = source(turn) // 2
+        return i, [
+            remote(
+                transit.at[i], keys.at[slot], g_send.at[2 * turn + n], key_sem.at[slot],
+                ((row * NZ) + z, head),
+            )
+            for n, row in enumerate((3 - y, 3 - beside))
+        ]
+
+    for turn in range(4):
+        @pl.when(passing)
+        def _():
+            i, copies = passed(turn)
+            remote(transit.at[i], transit.at[i], g_send.at[2 * turn], tr_sem.at[i], partner).wait_recv()
+            for copy in copies:
                 copy.start()
+
+        @pl.when(active)
+        def _():
+            first, relay = forwards(turn)
             first.wait_recv()
             first.start()
             relay.start()
@@ -225,33 +239,31 @@
     @pl.when(active)
     def _():
         for turn in range(4):
-            i = arrival(turn)
-            for n in range(3):
-                other = y // 2 * 2 + 1 - y % 2 if n == 0 else far_row + n - 1
-                slot = other * NZ + 2 * i + c
-                relay = key_copy(slot, r_send.at[4 + 3 * turn + n], sibling)
+            for n, row in enumerate((beside, 3 - y, 3 - beside)):
+                relay = key_copy(row * NZ + source(turn), r_send.at[4 + 3 * turn + n], sibling)
                 relay.wait_recv()
                 relay.start()
         for i in range(4):
             for row in range(NY):
-                slot = row * NZ + 2 * i + 1 - c
-                key_copy(slot, r_send.at[0], sibling).wait_recv()
-        for i in range(4):
-            first, relay, others = forwards(i)
-            first.wait_send()
-            relay.wait_send()
-            for copy in others:
+                key_copy(row * NZ + 2 * i + 1 - c, r_send.at[0], sibling).wait_recv()
+        for turn in range(4):
+            key_copy(0, f_send.at[turn], partner).wait_send()
+        for n in range(16):
+            key_copy(0, r_send.at[n], sibling).wait_send()
+
+    @pl.when(passing)
+    def _():
+        for turn in range(4):
+            for copy in passed(turn)[1]:
                 copy.wait_send()
-            for n in range(3):
-                key_copy(0, r_send.at[4 + 3 * i + n], sibling).wait_send()
 
     for d in range(1, 8):
         other = (head + d) % 8
         remote(cols.at[other], cols.at[other], h_send.at[d], h_recv.at[other], sibling).wait_recv()
     for copy in head_outs + column_outs + outs:
         copy.wait_send()
-    for k in order[NZ - 1 - FLIGHT :]:
-        send_piece(k, False)
+    for to in order[NZ - 1 - FLIGHT :]:
+        send_piece(to, False)
 
 
 def spread(t_shift, s_shift, tq, tk, tv, hidden, wq, wk, wv):
@@ -268,18 +280,16 @@
         in_specs=[smem, smem] + [anywhere] * 7,
         out_specs=(anywhere, anywhere),
         scratch_shapes=[
-            pltpu.VMEM((3, TOK, 512), BF16),
+            pltpu.VMEM((PAIRS, TOK, 512), BF16),
             pltpu.VMEM((TOK, 2048), BF16),
             pltpu.VMEM((3, 2048, 128), BF16),
-            pltpu.VMEM((3, TOK, 128), BF16),
-            pltpu.VMEM((3, TOK, 128), BF16),
             pltpu.VMEM((TOK, 384), BF16),
             pltpu.VMEM((TOK, 384), BF16),
             pltpu.VMEM((TOK, 384), BF16),
             pltpu.VMEM((NZ, PIECE, 128), BF16),
             pltpu.VMEM((4, PIECE, 128), BF16),
             pltpu.VMEM((4, 128, TOK), BF16),
-            dma((7,)), dma((4,)), dma((4,)), dma((4,)), dma((4,)),
+            dma((10,)), dma((4,)), dma((4,)), dma((4,)), dma((4,)),
             dma((NZ,)), dma((SLOTS,)), dma((4,)), dma((4,)), dma((8,)), dma((16,)),
             dma((4,)), dma((4,)), dma((8,)), dma((8,)),
         ],
@@ -298,24 +308,23 @@
     return tile.astype(BF16)
 
 
-def relate_kernel(
-    lengths, keys, part, div, kt, kst, st, ss, acc, top_t, top_s, row_t, row_s, cross, begin, load
-):
+def relate_kernel(lengths, keys, part, kt, kst, ks, st, ss, acc, load):
     _, _, y, z, _, c = place()
     group = 2 * (y % 2) + c
-    div[...] = jnp.zeros_like(div)
     coef = jnp.float32(1.0 / 48.0)
     scale = jnp.float32(1.0 / 16.0)
     scale2 = jnp.float32(math.log2(math.e) / 16.0)
     span = CHUNK // TOK
+    two = ROWS // TOK
     blocks = KEYS // ROWS
-
-    @pl.when(z < PAIRS)
+    last_dims = (((1,), (1,)), ((), ()))
+
+    @pl.when(pair_at(z, y // 2) < PAIRS)
     def _():
         loads = [
+            pltpu.make_async_copy(keys.at[:, 256:320], kst, load.at[2]),
             pltpu.make_async_copy(keys.at[:, 0:128], kt.at[:, :, 0:128], load.at[0]),
             pltpu.make_async_copy(keys.at[:, 128:256], kt.at[:, :, 128:256], load.at[1]),
-            pltpu.make_async_copy(keys.at[:, 256:320], kst, load.at[2]),
         ]
         for copy in loads:
             copy.start()
@@ -335,11 +344,24 @@
             lengths[0] == most, end0, jnp.where(lengths[1] == most, end1, jnp.where(lengths[2] == most, end2, KEYS))
         )
         last_block = (last - 1) // ROWS
-        for copy in loads:
+        unit = jnp.where(
+            lax.broadcasted_iota(jnp.int32, (TOK, TOK), 0) == lax.broadcasted_iota(jnp.int32, (TOK, TOK), 1),
+            jnp.float32(1.0),
+            jnp.float32(0.0),
+        ).astype(BF16)
+        loads[0].wait()
+
+        @pl.loop(0, SLOTS // 4)
+        def _(n):
+            for u in range(4):
+                ks[4 * n + u] = lax.dot_general(
+                    unit, kst[4 * n + u], last_dims, preferred_element_type=F32
+                ).astype(BF16)
+
+        for copy in loads[1:]:
             copy.wait()
 
-        @pl.loop(0, 4)
-        def _(t):
+        def one_block(t, div):
             odd = t % 2
             nth = 4 * t + odd * 3 + (1 - 2 * odd) * group
             block = (last_block + blocks - nth) % blocks
@@ -347,122 +369,99 @@
             lower = first_of(r0) // CHUNK
             upper = (r0 + ROWS - 1) // CHUNK + 1
             latest = first_of(r0 + ROWS - 1)
-            top_t[...] = jnp.full_like(top_t, NEG)
-            top_s[...] = jnp.full_like(top_s, NEG)
-            begin[...] = first_of(r0 + lax.broadcasted_iota(jnp.int32, (ROWS, 128), 0))
-            two = ROWS // TOK
+            row = r0 + lax.broadcasted_iota(jnp.int32, (8, ROWS), 1)
+            start = first_of(row)
+            sub_row = lax.broadcasted_iota(jnp.int32, (8, ROWS), 0)
             bt = jnp.concatenate([kst[block * two + u] for u in range(two)], axis=1)
-            b2 = (jnp.transpose(bt.astype(F32)) * jnp.float32(2.0)).astype(BF16)
-
-            def key_columns(n):
-                return jnp.concatenate([kst[n * span + u] for u in range(span)], axis=1)
-
-            def scores(n):
+            b2 = (bt.astype(F32) * jnp.float32(2.0)).astype(BF16)
+
+            def online(n, carry, mask):
+                mt, ms, tot_t, tot_s, cross = carry
+                k0 = pl.multiple_of(n * CHUNK, CHUNK)
                 a = lax.dot_general(
+                    kt[pl.ds(n * span, span)].reshape(CHUNK, 256),
                     kt[pl.ds(block * two, two)].reshape(ROWS, 256),
-                    kt[pl.ds(n * span, span)].reshape(CHUNK, 256),
-                    (((1,), (1,)), ((), ())),
+                    last_dims,
                     preferred_element_type=F32,
                 )
-                return a, jnp.dot(b2, key_columns(n), preferred_element_type=F32)
-
-            def online(n, a, b, allowed):
-                k0 = pl.multiple_of(n * CHUNK, CHUNK)
-                for r in range(0, ROWS, SUB):
-                    rows = slice(r, r + SUB)
-                    xs = []
-                    ws = []
-                    for q in range(span):
-                        x = a[rows, q * 128 : q * 128 + 128]
-                        w = b[rows, q * 128 : q * 128 + 128]
-                        if allowed is not None:
-                            keep = allowed(k0 + q * 128, r)
-                            x = jnp.where(keep, x, NEG)
-                            w = jnp.where(keep, w, NEG)
-                        at = pl.ds(pl.multiple_of(k0 + q * 128, 128), 128)
-                        st[rows, at] = x
-                        ss[rows, at] = w
+                b = jnp.dot(ks[pl.ds(n * span, span)].reshape(CHUNK, 64), b2, preferred_element_type=F32)
+                for first in range(0, CHUNK, 64):
+                    xs, ws = [], []
+                    new_t, new_s = mt, ms
+                    for g in range(first, first + 64, 8):
+                        x = a[g : g + 8]
+                        w = b[g : g + 8]
+                        if mask:
+                            column = sub_row + (k0 + g)
+                            allowed = jnp.logical_and(column >= start, column <= row)
+                            x = jnp.where(allowed, x, NEG)
+                            w = jnp.where(allowed, w, NEG)
+                        st[pl.ds(pl.multiple_of(k0 + g, 8), 8)] = x
+                        ss[pl.ds(pl.multiple_of(k0 + g, 8), 8)] = w
+                        new_t = jnp.maximum(new_t, x)
+                        new_s = jnp.maximum(new_s, w)
                         xs.append(x)
                         ws.append(w)
-                    old_t = top_t[rows]
-                    old_s = top_s[rows]
-                    mt = functools.reduce(jnp.maximum, xs, old_t)
-                    ms = functools.reduce(jnp.maximum, ws, old_s)
-                    top_t[rows] = mt
-                    top_s[rows] = ms
-                    fade = jnp.exp2((old_t - mt) * scale2)
-                    tot_t = row_t[rows] * fade
-                    mix = cross[rows] * fade
-                    tot_s = row_s[rows] * jnp.exp2((old_s - ms) * scale2)
+                    fade = jnp.exp2((mt - new_t) * scale2)
+                    tot_t = tot_t * fade
+                    cross = cross * fade
+                    tot_s = tot_s * jnp.exp2((ms - new_s) * scale2)
+                    mt, ms = new_t, new_s
                     for x, w in zip(xs, ws):
                         ea = jnp.exp2((x - mt) * scale2)
                         tot_t = tot_t + ea
                         tot_s = tot_s + jnp.exp2((w - ms) * scale2)
-                        mix = mix + ea * (x - w)
-                    row_t[rows] = tot_t
-                    row_s[rows] = tot_s
-                    cross[rows] = mix
-
-            def masked(n):
-                def allowed(c0, r):
-                    row = r0 + r + lax.broadcasted_iota(jnp.int32, (SUB, 128), 0)
-                    column = c0 + lax.broadcasted_iota(jnp.int32, (SUB, 128), 1)
-                    return jnp.logical_and(column >= begin[r : r + SUB], column <= row)
-
-                online(n, *scores(n), allowed)
-
-            def whole(n):
-                online(n, *scores(n), None)
-
-            row_t[...] = jnp.zeros_like(row_t)
-            row_s[...] = jnp.zeros_like(row_s)
-            cross[...] = jnp.zeros_like(cross)
+                        cross = cross + ea * (x - w)
+                return mt, ms, tot_t, tot_s, cross
+
             inner = jnp.minimum((latest + CHUNK - 1) // CHUNK, upper)
             outer = jnp.maximum((r0 + 1) // CHUNK, inner)
-
-            @pl.loop(0, upper - lower - (outer - inner))
-            def _(n):
-                masked(jnp.where(lower + n < inner, lower + n, lower + n + (outer - inner)))
-
-            @pl.loop(inner, outer)
-            def _(n):
-                whole(n)
-
-            mt = jnp.max(top_t[...], axis=1, keepdims=True)
-            ms = jnp.max(top_s[...], axis=1, keepdims=True)
-            fade = jnp.exp2((top_t[...] - mt) * scale2)
-            tot_t = jnp.sum(row_t[...] * fade, axis=1, keepdims=True)
-            tot_s = jnp.sum(row_s[...] * jnp.exp2((top_s[...] - ms) * scale2), axis=1, keepdims=True)
-            mixed = jnp.sum(cross[...] * fade, axis=1, keepdims=True)
-            value = (mixed / tot_t + (ms - mt)) * scale + (jnp.log(tot_s) - jnp.log(tot_t))
-            wide = jnp.broadcast_to(value * jnp.float32(1.0 / 128.0), (ROWS, 128))
-            div[...] += jnp.sum(wide.reshape(ROWS // 8, 8, 128), axis=0)
-            top_t[...] = jnp.broadcast_to(mt, (ROWS, 128))
-            top_s[...] = jnp.broadcast_to(ms, (ROWS, 128))
-            row_t[...] = jnp.broadcast_to(jnp.log2(coef / tot_t), (ROWS, 128))
-            row_s[...] = jnp.broadcast_to(jnp.log2(coef / tot_s), (ROWS, 128))
+            low = jnp.full((8, ROWS), NEG, F32)
+            zero = jnp.zeros((8, ROWS), F32)
+            carry = lax.fori_loop(
+                0,
+                upper - lower - (outer - inner),
+                lambda n, carry: online(
+                    jnp.where(lower + n < inner, lower + n, lower + n + (outer - inner)), carry, True
+                ),
+                (low, low, zero, zero, zero),
+            )
+            mt, ms, tot_t, tot_s, cross = lax.fori_loop(
+                inner, outer, lambda n, carry: online(n, carry, False), carry
+            )
+            top_t = jnp.max(mt, axis=0, keepdims=True)
+            top_s = jnp.max(ms, axis=0, keepdims=True)
+            fade = jnp.exp2((mt - top_t) * scale2)
+            tot_t = jnp.sum(tot_t * fade, axis=0, keepdims=True)
+            tot_s = jnp.sum(tot_s * jnp.exp2((ms - top_s) * scale2), axis=0, keepdims=True)
+            mixed = jnp.sum(cross * fade, axis=0, keepdims=True)
+            value = (mixed / tot_t + (top_s - top_t)) * scale + (jnp.log(tot_s) - jnp.log(tot_t))
+            div = div + value[:, 0:128] + value[:, 128:256]
+            log_t = jnp.log2(coef / tot_t)
+            log_s = jnp.log2(coef / tot_s)
 
             def gradient(n, near):
                 k0 = pl.multiple_of(n * CHUNK, CHUNK)
-                columns = []
-                for q in range(span):
-                    at = pl.ds(pl.multiple_of(k0 + q * 128, 128), 128)
-                    columns.append(
+                pieces = []
+                for g in range(0, CHUNK, 64):
+                    at = pl.ds(pl.multiple_of(k0 + g, 64), 64)
+                    pieces.append(
                         (
-                            jnp.exp2((ss[:, at] - top_s[...]) * scale2 + row_s[...])
-                            - jnp.exp2((st[:, at] - top_t[...]) * scale2 + row_t[...])
+                            jnp.exp2((ss[at] - top_s) * scale2 + log_s)
+                            - jnp.exp2((st[at] - top_t) * scale2 + log_t)
                         ).astype(BF16)
                     )
-                g = jnp.concatenate(columns, axis=1)
-                acc[:, pl.ds(k0, CHUNK)] += jnp.dot(bt, g, preferred_element_type=F32)
-                return near + lax.dot_general(
-                    key_columns(n), g, (((1,), (1,)), ((), ())), preferred_element_type=F32
-                )
+                g = jnp.concatenate(pieces, axis=0)
+                columns = jnp.concatenate([kst[n * span + u] for u in range(span)], axis=1)
+                acc[:, pl.ds(k0, CHUNK)] += lax.dot_general(bt, g, last_dims, preferred_element_type=F32)
+                return near + jnp.dot(columns, g, preferred_element_type=F32)
 
             near = lax.fori_loop(lower, upper, gradient, jnp.zeros((64, ROWS), F32))
             acc[:, pl.ds(pl.multiple_of(r0, ROWS), ROWS)] += near
-
-        tile = in_three(jnp.sum(div[...], axis=0, keepdims=True))
+            return div
+
+        div = lax.fori_loop(0, 4, one_block, jnp.zeros((1, 128), F32))
+        tile = in_three(div)
         for row in range(NY):
             for parity in range(2):
                 for i in range(4):
@@ -479,24 +478,16 @@
     return pl.pallas_call(
         relate_kernel,
         name="relate",
-        out_shape=(
-            jax.ShapeDtypeStruct((NY, 2, PART, 128), BF16)
-        ),
+        out_shape=jax.ShapeDtypeStruct((NY, 2, PART, 128), BF16),
         in_specs=[smem, pl.BlockSpec(memory_space=pl.ANY)],
         out_specs=vmem,
         scratch_shapes=[
-            pltpu.VMEM((8, 128), F32),
             pltpu.VMEM((SLOTS, TOK, 256), BF16),
             pltpu.VMEM((SLOTS, 64, TOK), BF16),
-            pltpu.VMEM((ROWS, KEYS), F32),
-            pltpu.VMEM((ROWS, KEYS), F32),
+            pltpu.VMEM((SLOTS, TOK, 64), BF16),
+            pltpu.VMEM((KEYS, ROWS), F32),
+            pltpu.VMEM((KEYS, ROWS), F32),
             pltpu.VMEM((64, KEYS), F32),
-            pltpu.VMEM((ROWS, 128), F32),
-            pltpu.VMEM((ROWS, 128), F32),
-            pltpu.VMEM((ROWS, 128), F32),
-            pltpu.VMEM((ROWS, 128), F32),
-            pltpu.VMEM((ROWS, 128), F32),
-            pltpu.VMEM((ROWS, 128), jnp.int32),
             pltpu.SemaphoreType.DMA((3,)),
         ],
         compiler_params=pltpu.CompilerParams(vmem_limit_bytes=VMEM_LIMIT),
@@ -523,7 +514,7 @@
             peers.append((((y + dy) % NY) * NZ + z, h))
         peers.append((((y + dy) % NY) * NZ + z + 1 - 2 * (z % 2), head))
     greet(peers)()
-    active = z < PAIRS
+    active = pair_at(z, y // 2) < PAIRS
 
     def row_copies():
         me = y * 2 + c
@@ -544,9 +535,10 @@
         pltpu.make_async_copy(part.at[y, c], in1.at[y * 2 + c], r1.at[y * 2 + c]).start()
 
     def each_pair_copy(p, go):
+        k = pair_at(z, p)
         for i in range(4):
-            copy = remote(sums.at[p], in2.at[z], s2.at[p * 4 + i], r2.at[z], (y * NZ + 2 * i + c, 2 * x + p))
-            mine = jnp.logical_and(z == 2 * i + c, c == p)
+            copy = remote(sums.at[p], in2.at[k], s2.at[p * 4 + i], r2.at[k], (y * NZ + 2 * i + c, 2 * x + p))
+            mine = jnp.logical_and(c == p, z == 2 * i + c)
 
             @pl.when(jnp.logical_not(mine))
             def _():
@@ -555,11 +547,11 @@
             if go:
                 @pl.when(mine)
                 def _():
-                    pltpu.make_async_copy(sums.at[p], in2.at[z], r2.at[z]).start()
-
-    @pl.when(active)
-    def _():
-        for p in range(2):
+                    pltpu.make_async_copy(sums.at[p], in2.at[k], r2.at[k]).start()
+
+    for p in range(2):
+        @pl.when(pair_at(z, p) < PAIRS)
+        def _():
             total = jnp.zeros((256, 128), F32)
             tiles = jnp.zeros((16, 128), F32)
             for n in range(4 * p, 4 * p + 4):
@@ -574,11 +566,12 @@
     tiles = jnp.zeros((16, 128), F32)
     for k in range(PAIRS):
         pltpu.make_async_copy(in2.at[k], in2.at[k], r2.at[k]).wait()
+    for k in range(PAIRS):
         tiles = tiles + in2[k, 256:PART].astype(F32)
     grad = jnp.zeros((512, 384), F32)
     for i in range(4):
         grad = grad + lax.dot_general(
-            fetched[:, i].reshape(512, TOK), in2[:, i * 64 : (i + 1) * 64].reshape(384, TOK),
+            fetched[:, i].reshape(512, TOK), in2[0:PAIRS, i * 64 : (i + 1) * 64].reshape(384, TOK),
             (((1,), (1,)), ((), ())),
             preferred_element_type=F32,
         )
@@ -621,7 +614,10 @@
     def _():
         for copy in row_copies():
             copy.wait_send()
-        for p in range(2):
+
+    for p in range(2):
+        @pl.when(pair_at(z, p) < PAIRS)
+        def _():
             each_pair_copy(p, False)
 
     total = jnp.zeros((8, 128), F32)
@@ -649,7 +645,7 @@
         scratch_shapes=[
             pltpu.VMEM((8, PART, 128), BF16),
             pltpu.VMEM((2, PART, 128), BF16),
-            pltpu.VMEM((PAIRS, PART, 128), BF16),
+            pltpu.VMEM((NZ, PART, 128), BF16),
             pltpu.VMEM((8, 64, 384), BF16),
             pltpu.VMEM((8, 64, 384), BF16),
             pltpu.VMEM((64, 384), BF16),
@@ -658,7 +654,7 @@
             pltpu.VMEM((8, 8, 128), F32),
             pltpu.VMEM((8, 128), F32),
             pltpu.VMEM((8, 4, 64, TOK), BF16),
-            dma(()), dma((8,)), dma((8,)), dma((8,)), dma((PAIRS,)), dma((8,)), dma((8,)),
+            dma(()), dma((8,)), dma((8,)), dma((8,)), dma((NZ,)), dma((8,)), dma((8,)),
             dma(()), dma(()), dma(()), dma(()), dma((8,)), dma((8,)),
         ],
         compiler_params=pltpu.CompilerParams(

time: 99.1 us -> 95.2 us (0.961)
  Pallas kernels: 95.2 us -> 91.1 us
    pallas_call x1, Pallas kernels: 36.1 us -> 33 us  [fold(): pl.pallas_call(fold_kernel, name='fold', out_shape=(jax.ShapeDtypeStruct(...]
    pallas_call x1, Pallas kernels: 17.2 us -> 15.2 us  [relate(): pl.pallas_call(relate_kernel, name='relate', out_shape=jax.ShapeDtypeStru...]
where the time goes in v3:
time: 95.2 us; the launch traced here: 94.8 us
  Pallas kernels  91.1 us (96%)
  between operations  3.7 us (4%)
    pallas_call x1, Pallas kernels, spread(): pl.pallas_call(spread_kernel, name='spread', out_shape=(jax.ShapeDtypeStr...  41.2 us
    pallas_call x1, Pallas kernels, fold(): pl.pallas_call(fold_kernel, name='fold', out_shape=(jax.ShapeDtypeStruct(...  33 us
    pallas_call x1, Pallas kernels, relate(): pl.pallas_call(relate_kernel, name='relate', out_shape=jax.ShapeDtypeStru...  15.2 us

profile of v3, /device:TPU:1, one launch (start us, length us, event | category | flops | bytes accessed | tf_op | source)
XLA Modules:
  0.0 94.8 jit_solution(11367034273746738213)
XLA Ops:
  1.9 41.2 %spread.1 = (bf16[32,320,128]{2,1,0:T(8,128)(2,1)}, bf16[8,4,64,128]{3,2,1,0:T(8,128)(2,1)}) custom-call(s32[1]{0:T(128)S(6)} %copy.15.t_shift, s32[1]{0:T(128)S(6)} %copy.16.s_shift, bf16[128,512]{1,0:T(8,128)(2,1)} %tq.1, bf16[128,512]{1,0:T(8,128)(2,1)} %tk.1, bf16[128,512]{1,0:T(8,128)(2,1)} %tv.1, bf16[128,2048]{1,0:T(8,128)(2,1)} %hidden.1, ...), custom_call_target="tpu_custom_call" | custom-call | tf_op jit(solution)/shard_map/spread/pallas_call | solution.py:273
  43.1 15.2 %relate.1.part = bf16[4,2,272,128]{3,2,1,0:T(8,128)(2,1)} custom-call(s32[4]{0:T(128)} %lengths.1, bf16[32,320,128]{2,1,0:T(8,128)(2,1)} %get-tuple-element.11.keys), custom_call_target="tpu_custom_call" | custom-call | tf_op jit(solution)/shard_map/relate/pallas_call | solution.py:478
  58.3 33.0 %fold.1 = (f32[1,1]{1,0:T(1,128)}, bf16[64,1152]{1,0:T(8,128)(2,1)}) custom-call(bf16[4,2,272,128]{3,2,1,0:T(8,128)(2,1)} %relate.1.part, bf16[8,4,64,128]{3,2,1,0:T(8,128)(2,1)} %get-tuple-element.12.cols), custom_call_target="tpu_custom_call" | custom-call | tf_op jit(solution)/shard_map/fold/pallas_call | solution.py:639
  91.3 1.7 %shift.1 = (bf16[64,128]{1,0:T(8,128)(2,1)}, bf16[64,128]{1,0:T(8,128)(2,1)}, bf16[64,128]{1,0:T(8,128)(2,1)}) custom-call(s32[1]{0:T(128)S(6)} %copy.16.s_shift, bf16[64,1152]{1,0:T(8,128)(2,1)} %get-tuple-element.14.both), custom_call_target="tpu_custom_call" | custom-call | tf_op jit(solution)/shard_map/shift/pallas_call | solution.py:687

commit v4 on v3

--- a/solution.py
+++ b/solution.py
@@ -102,7 +102,7 @@
         outs.append(remote(last, stack.at[2 * kind, :, 0:128], p_send.at[kind], p_recv.at[kind], ahead))
     outs.append(remote(stud, small_n, n_send.at[3], n_recv.at[3], behind))
     outs.append(remote(stud, small_p, p_send.at[3], p_recv.at[3], ahead))
-    for copy in outs:
+    for copy in outs[6:] + outs[:6]:
         copy.start()
 
     for part in range(4):
@@ -158,14 +158,6 @@
                 pltpu.make_async_copy(piece.at[k], transit.at[z // 2], tr_sem.at[z // 2]).start()
 
     transposed = (((1,), (1,)), ((), ()))
-    for copy in loads[4:]:
-        copy.wait()
-    for copy in outs[:6]:
-        copy.wait_recv()
-    window = jnp.dot(stack[...].reshape(PAIRS * TOK, 512), pick_t, preferred_element_type=F32)
-    for k in range(PAIRS):
-        piece[k, 0:128] = window[k * TOK : (k + 1) * TOK, 0:128].astype(BF16)
-        piece[k, 128:256] = window[k * TOK : (k + 1) * TOK, 128:256].astype(BF16)
     for copy in outs[6:]:
         copy.wait_recv()
     for k in range(PAIRS):
@@ -176,6 +168,14 @@
             pick[:, 0:128], before[:, at], transposed, preferred_element_type=F32
         ) + lax.dot_general(pick[:, 128:256], after[:, at], transposed, preferred_element_type=F32)
         piece[k, 256:320] = small.astype(BF16)
+    for copy in loads[4:]:
+        copy.wait()
+    for copy in outs[:6]:
+        copy.wait_recv()
+    window = jnp.dot(stack[...].reshape(PAIRS * TOK, 512), pick_t, preferred_element_type=F32)
+    for k in range(PAIRS):
+        piece[k, 0:128] = window[k * TOK : (k + 1) * TOK, 0:128].astype(BF16)
+        piece[k, 128:256] = window[k * TOK : (k + 1) * TOK, 128:256].astype(BF16)
     order = [(z + d + NZ) % NZ for d in (0, 1, -1, 2, -2, 3, -3, 4)]
     for n, to in enumerate(order):
         if n > FLIGHT:
@@ -314,7 +314,6 @@
     coef = jnp.float32(1.0 / 48.0)
     scale = jnp.float32(1.0 / 16.0)
     scale2 = jnp.float32(math.log2(math.e) / 16.0)
-    span = CHUNK // TOK
     two = ROWS // TOK
     blocks = KEYS // ROWS
     last_dims = (((1,), (1,)), ((), ()))
@@ -351,11 +350,11 @@
         ).astype(BF16)
         loads[0].wait()
 
-        @pl.loop(0, SLOTS // 4)
+        @pl.loop(0, SLOTS // 8)
         def _(n):
-            for u in range(4):
-                ks[4 * n + u] = lax.dot_general(
-                    unit, kst[4 * n + u], last_dims, preferred_element_type=F32
+            for u in range(8):
+                ks[8 * n + u] = lax.dot_general(
+                    unit, kst[8 * n + u], last_dims, preferred_element_type=F32
                 ).astype(BF16)
 
         for copy in loads[1:]:
@@ -366,8 +365,8 @@
             nth = 4 * t + odd * 3 + (1 - 2 * odd) * group
             block = (last_block + blocks - nth) % blocks
             r0 = block * ROWS
-            lower = first_of(r0) // CHUNK
-            upper = (r0 + ROWS - 1) // CHUNK + 1
+            lower = first_of(r0) // ROWS
+            upper = block + 1
             latest = first_of(r0 + ROWS - 1)
             row = r0 + lax.broadcasted_iota(jnp.int32, (8, ROWS), 1)
             start = first_of(row)
@@ -375,17 +374,18 @@
             bt = jnp.concatenate([kst[block * two + u] for u in range(two)], axis=1)
             b2 = (bt.astype(F32) * jnp.float32(2.0)).astype(BF16)
 
-            def online(n, carry, mask):
+            def online(n, carry, width, mask):
                 mt, ms, tot_t, tot_s, cross = carry
-                k0 = pl.multiple_of(n * CHUNK, CHUNK)
+                k0 = pl.multiple_of(n * ROWS, ROWS)
+                slots = pl.ds(n * two, width // TOK)
                 a = lax.dot_general(
-                    kt[pl.ds(n * span, span)].reshape(CHUNK, 256),
+                    kt[slots].reshape(width, 256),
                     kt[pl.ds(block * two, two)].reshape(ROWS, 256),
                     last_dims,
                     preferred_element_type=F32,
                 )
-                b = jnp.dot(ks[pl.ds(n * span, span)].reshape(CHUNK, 64), b2, preferred_element_type=F32)
-                for first in range(0, CHUNK, 64):
+                b = jnp.dot(ks[slots].reshape(width, 64), b2, preferred_element_type=F32)
+                for first in range(0, width, 64):
                     xs, ws = [], []
                     new_t, new_s = mt, ms
                     for g in range(first, first + 64, 8):
@@ -414,20 +414,20 @@
                         cross = cross + ea * (x - w)
                 return mt, ms, tot_t, tot_s, cross
 
-            inner = jnp.minimum((latest + CHUNK - 1) // CHUNK, upper)
-            outer = jnp.maximum((r0 + 1) // CHUNK, inner)
+            inner = jnp.minimum((latest + ROWS - 1) // ROWS, upper)
+            wide = (jnp.maximum(block, inner) - inner) // 2
+            narrow = upper - lower - 2 * wide
+
+            def nth_narrow(n):
+                return jnp.where(lower + n < inner, lower + n, lower + n + 2 * wide)
+
             low = jnp.full((8, ROWS), NEG, F32)
             zero = jnp.zeros((8, ROWS), F32)
             carry = lax.fori_loop(
-                0,
-                upper - lower - (outer - inner),
-                lambda n, carry: online(
-                    jnp.where(lower + n < inner, lower + n, lower + n + (outer - inner)), carry, True
-                ),
-                (low, low, zero, zero, zero),
+                0, narrow, lambda n, carry: online(nth_narrow(n), carry, ROWS, True), (low, low, zero, zero, zero)
             )
             mt, ms, tot_t, tot_s, cross = lax.fori_loop(
-                inner, outer, lambda n, carry: online(n, carry, False), carry
+                0, wide, lambda n, carry: online(inner + 2 * n, carry, CHUNK, False), carry
             )
             top_t = jnp.max(mt, axis=0, keepdims=True)
             top_s = jnp.max(ms, axis=0, keepdims=True)
@@ -440,10 +440,10 @@
             log_t = jnp.log2(coef / tot_t)
             log_s = jnp.log2(coef / tot_s)
 
-            def gradient(n, near):
-                k0 = pl.multiple_of(n * CHUNK, CHUNK)
+            def gradient(n, near, width):
+                k0 = pl.multiple_of(n * ROWS, ROWS)
                 pieces = []
-                for g in range(0, CHUNK, 64):
+                for g in range(0, width, 64):
                     at = pl.ds(pl.multiple_of(k0 + g, 64), 64)
                     pieces.append(
                         (
@@ -452,11 +452,14 @@
                         ).astype(BF16)
                     )
                 g = jnp.concatenate(pieces, axis=0)
-                columns = jnp.concatenate([kst[n * span + u] for u in range(span)], axis=1)
-                acc[:, pl.ds(k0, CHUNK)] += lax.dot_general(bt, g, last_dims, preferred_element_type=F32)
+                columns = jnp.concatenate([kst[n * two + u] for u in range(width // TOK)], axis=1)
+                acc[:, pl.ds(k0, width)] += lax.dot_general(bt, g, last_dims, preferred_element_type=F32)
                 return near + jnp.dot(columns, g, preferred_element_type=F32)
 
-            near = lax.fori_loop(lower, upper, gradient, jnp.zeros((64, ROWS), F32))
+            near = lax.fori_loop(
+                0, narrow, lambda n, near: gradient(nth_narrow(n), near, ROWS), jnp.zeros((64, ROWS), F32)
+            )
+            near = lax.fori_loop(0, wide, lambda n, near: gradient(inner + 2 * n, near, CHUNK), near)
             acc[:, pl.ds(pl.multiple_of(r0, ROWS), ROWS)] += near
             return div
 
@@ -466,10 +469,10 @@
             for parity in range(2):
                 for i in range(4):
                     base = (row * NZ + 2 * i + parity) * TOK
-                    part[row, parity, i * 64 : (i + 1) * 64] = (
+                    part[parity, row, i * 64 : (i + 1) * 64] = (
                         acc[:, base : base + TOK] * jnp.float32(1.0 / 8.0)
                     ).astype(BF16)
-                part[row, parity, 256:PART] = tile
+                part[parity, row, 256:PART] = tile
 
 
 def relate(lengths, keys):
@@ -478,7 +481,7 @@
     return pl.pallas_call(
         relate_kernel,
         name="relate",
-        out_shape=jax.ShapeDtypeStruct((NY, 2, PART, 128), BF16),
+        out_shape=jax.ShapeDtypeStruct((2, NY, PART, 128), BF16),
         in_specs=[smem, pl.BlockSpec(memory_space=pl.ANY)],
         out_specs=vmem,
         scratch_shapes=[
@@ -496,8 +499,8 @@
 
 def fold_kernel(
     part, cols, mean, both,
-    in1, sums, in2, outp, in4, win, prev, follow, div_x, div_1, fetched,
-    load, s1, r1, s2, r2, s4, r4, sw, rw, sv, rv, sx, rx,
+    own, in0, pre, in1, sums, in2, outp, in4, win, prev, follow, div_x, div_1, fetched,
+    load, l0, s0, r0, s1, r1, s2, r2, s4, r4, sw, rw, sv, rv, sx, rx,
 ):
     seq, head, y, z, x, c = place()
     ahead = (seq, (head + 1) % 8)
@@ -505,34 +508,41 @@
     other = head + 1 - 2 * c
     fetch = pltpu.make_async_copy(cols, fetched, load)
     fetch.start()
+    active = pair_at(z, y // 2) < PAIRS
+    mine = pltpu.make_async_copy(part.at[c], own, l0)
+
+    @pl.when(active)
+    def _():
+        mine.start()
+
     peers = [(seq, (head + d) % 8) for d in range(1, 8)]
     for dz in range(1, NZ):
         for h in (head, other):
             peers.append((y * NZ + (z + dz) % NZ, h))
     for dy in range(1, NY):
-        for h in (head, other):
-            peers.append((((y + dy) % NY) * NZ + z, h))
+        peers.append((((y + dy) % NY) * NZ + z, head))
         peers.append((((y + dy) % NY) * NZ + z + 1 - 2 * (z % 2), head))
     greet(peers)()
-    active = pair_at(z, y // 2) < PAIRS
-
-    def row_copies():
-        me = y * 2 + c
-        copies = []
-        for dy in (2, 1, 3):
-            row = (y + dy) % NY
-            for core in range(2):
-                copies.append(
-                    remote(part.at[row, core], in1.at[me], s1.at[2 * dy + core], r1.at[me], (row * NZ + z, 2 * x + core))
-                )
-        copies.append(remote(part.at[y, 1 - c], in1.at[me], s1.at[0], r1.at[me], (seq, other)))
-        return copies
+    across = remote(part.at[1 - c], in0, s0, r0, (seq, other))
+    row_copies = [
+        remote(pre.at[(y + dy) % NY], in1.at[y], s1.at[dy], r1.at[y], (((y + dy) % NY) * NZ + z, head))
+        for dy in (2, 1, 3)
+    ]
 
     @pl.when(active)
     def _():
-        for copy in row_copies():
-            copy.start()
-        pltpu.make_async_copy(part.at[y, c], in1.at[y * 2 + c], r1.at[y * 2 + c]).start()
+        across.start()
+        mine.wait()
+        across.wait_recv()
+        for turn in range(NY):
+            row = (y + (2, 1, 3, 0)[turn]) % NY
+            pre[row, 0:256] = (own[row, 0:256].astype(F32) + in0[row, 0:256].astype(F32)).astype(BF16)
+            tiles = own[row, 256:PART].astype(F32) + in0[row, 256:PART].astype(F32)
+            pre[row, 256:PART] = in_three(jnp.sum(tiles, axis=0, keepdims=True))
+            if turn < 3:
+                row_copies[turn].start()
+            else:
+                pltpu.make_async_copy(pre.at[y], in1.at[y], r1.at[y]).start()
 
     def each_pair_copy(p, go):
         k = pair_at(z, p)
@@ -554,7 +564,7 @@
         def _():
             total = jnp.zeros((256, 128), F32)
             tiles = jnp.zeros((16, 128), F32)
-            for n in range(4 * p, 4 * p + 4):
+            for n in range(2 * p, 2 * p + 2):
                 pltpu.make_async_copy(in1.at[n], in1.at[n], r1.at[n]).wait()
                 total = total + in1[n, 0:256].astype(F32)
                 tiles = tiles + in1[n, 256:PART].astype(F32)
@@ -612,7 +622,8 @@
 
     @pl.when(active)
     def _():
-        for copy in row_copies():
+        across.wait_send()
+        for copy in row_copies:
             copy.wait_send()
 
     for p in range(2):
@@ -643,7 +654,10 @@
         in_specs=[pl.BlockSpec(memory_space=pl.ANY)] * 2,
         out_specs=(smem, vmem),
         scratch_shapes=[
-            pltpu.VMEM((8, PART, 128), BF16),
+            pltpu.VMEM((NY, PART, 128), BF16),
+            pltpu.VMEM((NY, PART, 128), BF16),
+            pltpu.VMEM((NY, PART, 128), BF16),
+            pltpu.VMEM((NY, PART, 128), BF16),
             pltpu.VMEM((2, PART, 128), BF16),
             pltpu.VMEM((NZ, PART, 128), BF16),
             pltpu.VMEM((8, 64, 384), BF16),
@@ -654,7 +668,7 @@
             pltpu.VMEM((8, 8, 128), F32),
             pltpu.VMEM((8, 128), F32),
             pltpu.VMEM((8, 4, 64, TOK), BF16),
-            dma(()), dma((8,)), dma((8,)), dma((8,)), dma((NZ,)), dma((8,)), dma((8,)),
+            dma(()), dma(()), dma(()), dma(()), dma((NY,)), dma((NY,)), dma((8,)), dma((NZ,)), dma((8,)), dma((8,)),
             dma(()), dma(()), dma(()), dma(()), dma((8,)), dma((8,)),
         ],
         compiler_params=pltpu.CompilerParams(

time: 95.2 us -> 94.2 us (0.989)
  no operation moved by 1% of the time
where the time goes in v4:
time: 94.2 us; the launch traced here: 94 us
  Pallas kernels  90.3 us (96%)
  between operations  3.7 us (4%)
    pallas_call x1, Pallas kernels, spread(): pl.pallas_call(spread_kernel, name='spread', out_shape=(jax.ShapeDtypeStr...  40.9 us
    pallas_call x1, Pallas kernels, fold(): pl.pallas_call(fold_kernel, name='fold', out_shape=(jax.ShapeDtypeStruct(...  32.2 us
    pallas_call x1, Pallas kernels, relate(): pl.pallas_call(relate_kernel, name='relate', out_shape=jax.ShapeDtypeStru...  15.5 us

profile of v4, /device:TPU:1, one launch (start us, length us, event | category | flops | bytes accessed | tf_op | source)
XLA Modules:
  0.0 94.0 jit_solution(8077289932874794746)
XLA Ops:
  1.9 40.9 %spread.1 = (bf16[32,320,128]{2,1,0:T(8,128)(2,1)}, bf16[8,4,64,128]{3,2,1,0:T(8,128)(2,1)}) custom-call(s32[1]{0:T(128)S(6)} %copy.15.t_shift, s32[1]{0:T(128)S(6)} %copy.16.s_shift, bf16[128,512]{1,0:T(8,128)(2,1)} %tq.1, bf16[128,512]{1,0:T(8,128)(2,1)} %tk.1, bf16[128,512]{1,0:T(8,128)(2,1)} %tv.1, bf16[128,2048]{1,0:T(8,128)(2,1)} %hidden.1, ...), custom_call_target="tpu_custom_call" | custom-call | tf_op jit(solution)/shard_map/spread/pallas_call | solution.py:273
  42.8 15.5 %relate.1.part = bf16[2,4,272,128]{3,2,1,0:T(8,128)(2,1)} custom-call(s32[4]{0:T(128)} %lengths.1, bf16[32,320,128]{2,1,0:T(8,128)(2,1)} %get-tuple-element.11.keys), custom_call_target="tpu_custom_call" | custom-call | tf_op jit(solution)/shard_map/relate/pallas_call | solution.py:481
  58.3 32.2 %fold.1 = (f32[1,1]{1,0:T(1,128)}, bf16[64,1152]{1,0:T(8,128)(2,1)}) custom-call(bf16[2,4,272,128]{3,2,1,0:T(8,128)(2,1)} %relate.1.part, bf16[8,4,64,128]{3,2,1,0:T(8,128)(2,1)} %get-tuple-element.12.cols), custom_call_target="tpu_custom_call" | custom-call | tf_op jit(solution)/shard_map/fold/pallas_call | solution.py:650
  90.5 1.7 %shift.1 = (bf16[64,128]{1,0:T(8,128)(2,1)}, bf16[64,128]{1,0:T(8,128)(2,1)}, bf16[64,128]{1,0:T(8,128)(2,1)}) custom-call(s32[1]{0:T(128)S(6)} %copy.16.s_shift, bf16[64,1152]{1,0:T(8,128)(2,1)} %get-tuple-element.14.both), custom_call_target="tpu_custom_call" | custom-call | tf_op jit(solution)/shard_map/shift/pallas_call | solution.py:701

commit v5 on v4

--- a/solution.py
+++ b/solution.py
@@ -62,7 +62,7 @@
     teachers = (tq, tk, tv)
     loads = [pltpu.make_async_copy(hidden, tokens, load.at[0])]
     for kind, weight in enumerate((wq, wk, wv)):
-        loads.append(pltpu.make_async_copy(weight, weights.at[kind], load.at[1 + kind]))
+        loads.append(pltpu.make_async_copy(weight, weights.at[:, kind * 128 : (kind + 1) * 128], load.at[1 + kind]))
     for kind in range(3):
         for j in range(2):
             loads.append(
@@ -84,12 +84,6 @@
         peers.append((((y + dy) % NY) * NZ + z, head))
     wait_all = greet(peers)
 
-    loads[0].wait()
-    for kind in range(3):
-        loads[1 + kind].wait()
-        stud[:, kind * 128 : (kind + 1) * 128] = jnp.dot(
-            tokens[...], weights[kind], preferred_element_type=F32
-        ).astype(BF16)
     wait_all()
 
     ahead = (seq, (head + 1) % 8)
@@ -100,9 +94,22 @@
             remote(first, stack.at[2 * kind + 1, :, 384:512], n_send.at[kind], n_recv.at[kind], behind)
         )
         outs.append(remote(last, stack.at[2 * kind, :, 0:128], p_send.at[kind], p_recv.at[kind], ahead))
-    outs.append(remote(stud, small_n, n_send.at[3], n_recv.at[3], behind))
-    outs.append(remote(stud, small_p, p_send.at[3], p_recv.at[3], ahead))
-    for copy in outs[6:] + outs[:6]:
+    outs.append(remote(stud, small_n.at[:, 128:256], n_send.at[3], n_recv.at[3], behind))
+    outs.append(remote(stud, small_p.at[:, 0:128], p_send.at[3], p_recv.at[3], ahead))
+    for copy in outs[:6]:
+        copy.start()
+
+    loads[0].wait()
+    for copy in loads[1:4]:
+        copy.wait()
+    projected = jnp.dot(tokens[...], weights[...], preferred_element_type=F32)
+    for kind in range(3):
+        rows = slice(kind * TOK, (kind + 1) * TOK)
+        values = projected[:, kind * 128 : (kind + 1) * 128].astype(BF16)
+        stud[rows] = values
+        small_p[rows, 128:256] = values
+        small_n[rows, 0:128] = values
+    for copy in outs[6:]:
         copy.start()
 
     for part in range(4):
@@ -158,16 +165,6 @@
                 pltpu.make_async_copy(piece.at[k], transit.at[z // 2], tr_sem.at[z // 2]).start()
 
     transposed = (((1,), (1,)), ((), ()))
-    for copy in outs[6:]:
-        copy.wait_recv()
-    for k in range(PAIRS):
-        at = slice(k // 2 * 128, (k // 2 + 1) * 128)
-        before, after = (small_p, stud) if k % 2 == 0 else (stud, small_n)
-        pick = pick_s[k % 2]
-        small = lax.dot_general(
-            pick[:, 0:128], before[:, at], transposed, preferred_element_type=F32
-        ) + lax.dot_general(pick[:, 128:256], after[:, at], transposed, preferred_element_type=F32)
-        piece[k, 256:320] = small.astype(BF16)
     for copy in loads[4:]:
         copy.wait()
     for copy in outs[:6]:
@@ -176,6 +173,12 @@
     for k in range(PAIRS):
         piece[k, 0:128] = window[k * TOK : (k + 1) * TOK, 0:128].astype(BF16)
         piece[k, 128:256] = window[k * TOK : (k + 1) * TOK, 128:256].astype(BF16)
+    for copy in outs[6:]:
+        copy.wait_recv()
+    for j, joined in enumerate((small_p, small_n)):
+        small = lax.dot_general(pick_s[j], joined[...], transposed, preferred_element_type=F32)
+        for kind in range(3):
+            piece[2 * kind + j, 256:320] = small[:, kind * TOK : (kind + 1) * TOK].astype(BF16)
     order = [(z + d + NZ) % NZ for d in (0, 1, -1, 2, -2, 3, -3, 4)]
     for n, to in enumerate(order):
         if n > FLIGHT:
@@ -282,10 +285,10 @@
         scratch_shapes=[
             pltpu.VMEM((PAIRS, TOK, 512), BF16),
             pltpu.VMEM((TOK, 2048), BF16),
-            pltpu.VMEM((3, 2048, 128), BF16),
-            pltpu.VMEM((TOK, 384), BF16),
-            pltpu.VMEM((TOK, 384), BF16),
-            pltpu.VMEM((TOK, 384), BF16),
+            pltpu.VMEM((2048, 384), BF16),
+            pltpu.VMEM((3 * TOK, 256), BF16),
+            pltpu.VMEM((3 * TOK, 256), BF16),
+            pltpu.VMEM((3 * TOK, 128), BF16),
             pltpu.VMEM((NZ, PIECE, 128), BF16),
             pltpu.VMEM((4, PIECE, 128), BF16),
             pltpu.VMEM((4, 128, TOK), BF16),
@@ -361,8 +364,8 @@
             copy.wait()
 
         def one_block(t, div):
-            odd = t % 2
-            nth = 4 * t + odd * 3 + (1 - 2 * odd) * group
+            falling = jnp.logical_or(t == 1, t == 2)
+            nth = 4 * t + jnp.where(falling, 3 - group, group)
             block = (last_block + blocks - nth) % blocks
             r0 = block * ROWS
             lower = first_of(r0) // ROWS
@@ -546,9 +549,10 @@
 
     def each_pair_copy(p, go):
         k = pair_at(z, p)
-        for i in range(4):
-            copy = remote(sums.at[p], in2.at[k], s2.at[p * 4 + i], r2.at[k], (y * NZ + 2 * i + c, 2 * x + p))
-            mine = jnp.logical_and(c == p, z == 2 * i + c)
+        for turn in (2, 1, 3, 0):
+            to = (z // 2 + turn) % 4 * 2 + c
+            copy = remote(sums.at[p], in2.at[k], s2.at[p * 4 + turn], r2.at[k], (y * NZ + to, 2 * x + p))
+            mine = jnp.logical_and(c == p, z == to)
 
             @pl.when(jnp.logical_not(mine))
             def _():

time: 94.2 us -> 93.5 us (level)
  no operation moved by 1% of the time
where the time goes in v5:
time: 93.5 us; the launch traced here: 93.3 us
  Pallas kernels  89.6 us (96%)
  between operations  3.7 us (4%)
    pallas_call x1, Pallas kernels, spread(): pl.pallas_call(spread_kernel, name='spread', out_shape=(jax.ShapeDtypeStr...  40.7 us
    pallas_call x1, Pallas kernels, fold(): pl.pallas_call(fold_kernel, name='fold', out_shape=(jax.ShapeDtypeStruct(...  32.4 us
    pallas_call x1, Pallas kernels, relate(): pl.pallas_call(relate_kernel, name='relate', out_shape=jax.ShapeDtypeStru...  14.7 us

profile of v5, /device:TPU:1, one launch (start us, length us, event | category | flops | bytes accessed | tf_op | source)
XLA Modules:
  0.0 93.3 jit_solution(9510832347489448614)
XLA Ops:
  1.9 40.7 %spread.1 = (bf16[32,320,128]{2,1,0:T(8,128)(2,1)}, bf16[8,4,64,128]{3,2,1,0:T(8,128)(2,1)}) custom-call(s32[1]{0:T(128)S(6)} %copy.15.t_shift, s32[1]{0:T(128)S(6)} %copy.16.s_shift, bf16[128,512]{1,0:T(8,128)(2,1)} %tq.1, bf16[128,512]{1,0:T(8,128)(2,1)} %tk.1, bf16[128,512]{1,0:T(8,128)(2,1)} %tv.1, bf16[128,2048]{1,0:T(8,128)(2,1)} %hidden.1, ...), custom_call_target="tpu_custom_call" | custom-call | tf_op jit(solution)/shard_map/spread/pallas_call | solution.py:276
  42.7 14.7 %relate.1.part = bf16[2,4,272,128]{3,2,1,0:T(8,128)(2,1)} custom-call(s32[4]{0:T(128)} %lengths.1, bf16[32,320,128]{2,1,0:T(8,128)(2,1)} %get-tuple-element.11.keys), custom_call_target="tpu_custom_call" | custom-call | tf_op jit(solution)/shard_map/relate/pallas_call | solution.py:484
  57.4 32.4 %fold.1 = (f32[1,1]{1,0:T(1,128)}, bf16[64,1152]{1,0:T(8,128)(2,1)}) custom-call(bf16[2,4,272,128]{3,2,1,0:T(8,128)(2,1)} %relate.1.part, bf16[8,4,64,128]{3,2,1,0:T(8,128)(2,1)} %get-tuple-element.12.cols), custom_call_target="tpu_custom_call" | custom-call | tf_op jit(solution)/shard_map/fold/pallas_call | solution.py:654
  89.8 1.7 %shift.1 = (bf16[64,128]{1,0:T(8,128)(2,1)}, bf16[64,128]{1,0:T(8,128)(2,1)}, bf16[64,128]{1,0:T(8,128)(2,1)}) custom-call(s32[1]{0:T(128)S(6)} %copy.16.s_shift, bf16[64,1152]{1,0:T(8,128)(2,1)} %get-tuple-element.14.both), custom_call_target="tpu_custom_call" | custom-call | tf_op jit(solution)/shard_map/shift/pallas_call | solution.py:705

commit v6 on v4

--- a/solution.py
+++ b/solution.py
@@ -578,28 +578,29 @@
         pltpu.make_async_copy(in2.at[k], in2.at[k], r2.at[k]).wait()
     for k in range(PAIRS):
         tiles = tiles + in2[k, 256:PART].astype(F32)
-    grad = jnp.zeros((512, 384), F32)
-    for i in range(4):
-        grad = grad + lax.dot_general(
-            fetched[:, i].reshape(512, TOK), in2[0:PAIRS, i * 64 : (i + 1) * 64].reshape(384, TOK),
-            (((1,), (1,)), ((), ())),
-            preferred_element_type=F32,
-        )
-    for n in range(8):
-        outp[n] = grad[n * 64 : (n + 1) * 64].astype(BF16)
-
     slot = y * 2 + z % 2
     block_copies = []
-    for d in (4, 5, 2, 3, 6, 7, 1):
-        to = (slot + d) % 8
-        block_copies.append(
-            remote(
-                outp.at[to], in4.at[slot], s4.at[d], r4.at[slot],
+    for turn in (2, 1, 3, 0):
+        row = (y + turn) % NY
+        grad = jnp.zeros((128, 384), F32)
+        for i in range(4):
+            grad = grad + lax.dot_general(
+                fetched[pl.ds(2 * row, 2), i].reshape(128, TOK),
+                in2[0:PAIRS, i * 64 : (i + 1) * 64].reshape(384, TOK),
+                (((1,), (1,)), ((), ())),
+                preferred_element_type=F32,
+            )
+        outp[pl.ds(2 * row, 2)] = grad.reshape(2, 64, 384).astype(BF16)
+        for b in range(2):
+            to = 2 * row + (b if turn > 0 else 1 - z % 2)
+            if turn == 0 and b == 1:
+                continue
+            copy = remote(
+                outp.at[to], in4.at[slot], s4.at[2 * turn + b], r4.at[slot],
                 ((to // 2) * NZ + (z // 2) * 2 + to % 2, head),
             )
-        )
-    for copy in block_copies:
-        copy.start()
+            copy.start()
+            block_copies.append(copy)
     pltpu.make_async_copy(outp.at[slot], in4.at[slot], r4.at[slot]).start()
 
     div_1[...] = jnp.broadcast_to(jnp.sum(tiles, axis=0, keepdims=True), (8, 128))

time: 94.2 us -> 92 us (0.977); the launches traced: 94 us -> 93.1 us
  no operation moved by 1% of the time
where the time goes in v6:
time: 92 us; the launch traced here: 93.1 us
  Pallas kernels  89.4 us (97%)
  between operations  3.7 us (4%)
    pallas_call x1, Pallas kernels, spread(): pl.pallas_call(spread_kernel, name='spread', out_shape=(jax.ShapeDtypeStr...  40.9 us
    pallas_call x1, Pallas kernels, fold(): pl.pallas_call(fold_kernel, name='fold', out_shape=(jax.ShapeDtypeStruct(...  31.3 us
    pallas_call x1, Pallas kernels, relate(): pl.pallas_call(relate_kernel, name='relate', out_shape=jax.ShapeDtypeStru...  15.5 us

profile of v6, /device:TPU:1, one launch (start us, length us, event | category | flops | bytes accessed | tf_op | source)
XLA Modules:
  0.0 93.1 jit_solution(138766557607914209)
XLA Ops:
  1.9 40.9 %spread.1 = (bf16[32,320,128]{2,1,0:T(8,128)(2,1)}, bf16[8,4,64,128]{3,2,1,0:T(8,128)(2,1)}) custom-call(s32[1]{0:T(128)S(6)} %copy.15.t_shift, s32[1]{0:T(128)S(6)} %copy.16.s_shift, bf16[128,512]{1,0:T(8,128)(2,1)} %tq.1, bf16[128,512]{1,0:T(8,128)(2,1)} %tk.1, bf16[128,512]{1,0:T(8,128)(2,1)} %tv.1, bf16[128,2048]{1,0:T(8,128)(2,1)} %hidden.1, ...), custom_call_target="tpu_custom_call" | custom-call | tf_op jit(solution)/shard_map/spread/pallas_call | solution.py:273
  42.8 15.5 %relate.1.part = bf16[2,4,272,128]{3,2,1,0:T(8,128)(2,1)} custom-call(s32[4]{0:T(128)} %lengths.1, bf16[32,320,128]{2,1,0:T(8,128)(2,1)} %get-tuple-element.11.keys), custom_call_target="tpu_custom_call" | custom-call | tf_op jit(solution)/shard_map/relate/pallas_call | solution.py:481
  58.3 31.3 %fold.1 = (f32[1,1]{1,0:T(1,128)}, bf16[64,1152]{1,0:T(8,128)(2,1)}) custom-call(bf16[2,4,272,128]{3,2,1,0:T(8,128)(2,1)} %relate.1.part, bf16[8,4,64,128]{3,2,1,0:T(8,128)(2,1)} %get-tuple-element.12.cols), custom_call_target="tpu_custom_call" | custom-call | tf_op jit(solution)/shard_map/fold/pallas_call | solution.py:651
  89.6 1.7 %shift.1 = (bf16[64,128]{1,0:T(8,128)(2,1)}, bf16[64,128]{1,0:T(8,128)(2,1)}, bf16[64,128]{1,0:T(8,128)(2,1)}) custom-call(s32[1]{0:T(128)S(6)} %copy.16.s_shift, bf16[64,1152]{1,0:T(8,128)(2,1)} %get-tuple-element.14.both), custom_call_target="tpu_custom_call" | custom-call | tf_op jit(solution)/shard_map/shift/pallas_call | solution.py:702
